TPU v7x, 32 devices: a whole 2x2x4 slice. The times are simulated.
32 devices in a mesh: depth: 8 (over z, x), batch: 4 (over y, core).
Axes of the slice: x: 2, y: 2, z: 4, core: 2. Of those that a mesh axis runs over, the one named last changes fastest.
Arguments:
- cpoint_guess: float32 [8, 4, 32, 4096], P('depth', 'batch'), may hold values from -6 to 6
- adjoint_guess: float32 [8, 4, 32, 4096], P('depth', 'batch'), may hold values from -6 to 6
- weights: float32 [64, 32, 32], P('depth'), may hold values from -0.5 to 0.5
- biases: float32 [64, 32], P('depth'), may hold values from -3 to 3
- diffusion: float32 [32], replicated, may hold values from 0.02 to 0.25
- section_len: int32 [8], replicated, may hold values from 1 to 8, 24 in all
Outputs:
- states_out: float32 [8, 4, 32, 4096], P('depth', 'batch')
- adjoint_out: float32 [8, 4, 32, 4096], P('depth', 'batch')
- grad_weights: float32 [64, 32, 32], P('depth')
- grad_biases: float32 [64, 32], P('depth')
Inputs may be any that keep to these rules, and one draw needn't show every extreme that they name: `section_len`: each of the 8 sections holds 1 to 8 layers, 24 in all, and one section holds exactly 8.
All inputs are finite; a program needn't handle non-finite values.
Results may differ from a plain program's by a relative error of at most 0.0003.
Values sent between devices are 32-bit elements; how exact they have to be, the bound alone decides.
No kernel may reach another device: no remote copies, remote signals or barrier semaphores. Data moves between devices by JAX's collectives and lax.ppermute only.
A program may use at most 128 MiB of HBM per device.

v0:
```python
import jax
import jax.numpy as jnp
from jax import lax
from jax.sharding import PartitionSpec as P

IMG_H = 64
IMG_W = 64
MOST = 8


def from_behind(value, axis, steps):
    count = lax.axis_size(axis)
    initial, last = (max(0, -steps), min(count, count - steps))
    return lax.ppermute(value, axis, [(source, source + steps) for source in range(initial, last)])


def laplace(states):
    shaped = states.reshape(states.shape[:-1] + (IMG_H, IMG_W))
    padded = jnp.pad(shaped, [(0, 0)] * (shaped.ndim - 2) + [(1, 1), (1, 1)])
    beside_all = (
        padded[..., 2:, 1:-1]
        + padded[..., :-2, 1:-1]
        + padded[..., 1:-1, 2:]
        + padded[..., 1:-1, :-2]
    )
    return (beside_all - 4.0 * shaped).reshape(states.shape)


def apply_layer(states, matrix, offset, diffusion, factor):
    pre_act = (
        jnp.einsum("ij,bjp->bip", matrix, states, precision=lax.Precision.HIGHEST)
        + offset[None, :, None]
    )
    mixed = jnp.einsum("ji,bjp->bip", matrix, jnp.tanh(pre_act), precision=lax.Precision.HIGHEST)
    return states + (factor * diffusion)[None, :, None] * laplace(states) - factor * mixed


def fine_factor():
    return jnp.asarray(1.0, jnp.float32) / MOST


def section(states, matrices, offsets, diffusion, layer_count):
    factor = fine_factor()

    def advance(position, current):
        changed = apply_layer(current, matrices[position], offsets[position], diffusion, factor)
        return jnp.where(position < layer_count - 1, changed, current)

    relaxed = lax.fori_loop(0, MOST - 1, advance, states)
    final_slot = layer_count - 1
    return apply_layer(relaxed, matrices[final_slot], offsets[final_slot], diffusion, factor)


def coarse(states, matrix, offset, diffusion, layer_count):
    factor = layer_count.astype(jnp.float32) / MOST
    return apply_layer(states, matrix, offset, diffusion, factor)


def body(cpoint_guess, adjoint_guess, weights, biases, diffusion, section_len):
    own_index = lax.axis_index("depth")
    last_index = lax.axis_size("depth") - 1
    layer_count = section_len[own_index]
    guess_now = cpoint_guess[0]
    pushed = section(guess_now, weights, biases, diffusion, layer_count)
    arrived = from_behind(pushed, "depth", 1)
    cpoints = jnp.where(own_index == 0, guess_now, arrived)
    second = section(cpoints, weights, biases, diffusion, layer_count)
    anchor = coarse(cpoints, weights[0], biases[0], diffusion, layer_count)
    tau_local = second - anchor
    every_points, every_tau, every_mats, every_offs = (
        lax.all_gather(cpoints[None], "depth", axis=0, tiled=True),
        lax.all_gather(tau_local[None], "depth", axis=0, tiled=True),
        lax.all_gather(weights[:1], "depth", axis=0, tiled=True),
        lax.all_gather(biases[:1], "depth", axis=0, tiled=True),
    )

    def coarse_step(current, packed):
        mat, off, count_here, tau_here = packed
        return (coarse(current, mat, off, diffusion, count_here) + tau_here, current)

    _, every_states = lax.scan(
        coarse_step, every_points[0], (every_mats, every_offs, section_len, every_tau)
    )
    states_out = every_states[own_index]
    _, pullback = jax.vjp(
        lambda start_state: section(start_state, weights, biases, diffusion, layer_count), cpoints
    )
    lam_start = pullback(adjoint_guess[0])[0]
    from_next = from_behind(lam_start, "depth", -1)
    lam_end = jnp.where(own_index == last_index, adjoint_guess[0], from_next)
    _, pull_full = jax.vjp(
        lambda start_state, mat_all, off_all: section(
            start_state, mat_all, off_all, diffusion, layer_count
        ),
        cpoints,
        weights,
        biases,
    )
    adjoint_here, grad_mats, grad_offs = pull_full(lam_end)
    grad_mats, grad_offs = lax.psum((grad_mats, grad_offs), "batch")
    return (states_out[None], adjoint_here[None], grad_mats, grad_offs)


def solution(mesh):
    placed = (
        P("depth", "batch", None, None),
        P("depth", "batch", None, None),
        P("depth", None, None),
        P("depth", None),
        P(),
        P(),
    )
    return jax.shard_map(
        body,
        mesh=mesh,
        in_specs=placed,
        out_specs=(
            P("depth", "batch", None, None),
            P("depth", "batch", None, None),
            P("depth", None, None),
            P("depth", None),
        ),
        check_vma=False,
    )
```

profile of v0, /device:TPU:0, one launch (start us, length us, event | category | flops | bytes accessed | tf_op | source)
XLA Modules:
  0.0 650.3 jit_solution(15327682241678094067)
XLA Ops:
  10.8 34.7 %while.134 = (s32[]{:T(128)}, f32[1,32,4096]{2,1,0:T(8,128)S(1)}, s32[]{:T(128)}, f32[32]{0:T(128)}, f32[8,32,32]{2,1,0:T(8,128)}, /*index=5*/f32[8,32]{1,0:T(8,128)}, s32[]{:T(128)}) while((s32[]{:T(128)}, f32[1,32,4096]{2,1,0:T(8,128)S(1)}, s32[]{:T(128)}, f32[32]{0:T(128)}, f32[8,32,32]{2,1,0:T(8,128)}, /*index=5*/f32[8,32]{1,0:T(8,128)}, ...), condition=%wide.region_1.2_spmd, body=%wide.region_0.1_spmd.sunk | while | flops 102105120 | bytes 6325639 | solution.py:49
  53.1 5.6 collective-permute-start
  61.1 23.1 %all-gather.2 = f32[8,1,32]{2,1,0:T(1,128)S(1)} all-gather(f32[1,1,32]{2,1,0:T(1,128)S(1)} %get-tuple-element.1400), channel_id=1, replica_groups=mesh['depth'=8,'batch'=4] {'depth'}, dimensions={0}, use_global_device_ids=true | all-gather | bytes 1152 | tf_op jit(solution)/shard_map/all_gather | solution.py:74
  84.3 30.5 %all_gather.13 = f32[8,32,32]{2,1,0:T(8,128)S(1)} all-gather(f32[1,32,32]{2,1,0:T(8,128)S(1)} %slice.241), channel_id=1, replica_groups=mesh['depth'=8,'batch'=4] {'depth'}, dimensions={0}, use_global_device_ids=true | all-gather | bytes 36864 | tf_op jit(solution)/shard_map/all_gather | solution.py:73
  123.5 82.5 %while.137 = (s32[]{:T(128)}, f32[1,32,4096]{2,1,0:T(8,128)S(1)}, f32[7,32,32]{2,1,0:T(8,128)S(1)}, f32[7,1,32,4096]{3,2,1,0:T(8,128)}, pred[7]{0:T(512)(128)(4,...) while((s32[]{:T(128)}, f32[1,32,4096]{2,1,0:T(8,128)S(1)}, ...), condition=%wide.region_7.8_spmd, body=%wide.region_6.7_spmd.sunk | while | flops 102498304 | bytes 6883721 | solution.py:49
  127.2 4.0 fusion.331
  139.0 4.0 fusion.331
  150.7 4.0 fusion.331
  162.5 4.0 fusion.331
  174.3 4.0 fusion.331
  186.1 4.0 fusion.331
  197.9 4.0 fusion.331
  210.1 68.5 %while.138 = (s32[]{:T(128)}, f32[1,32,4096]{2,1,0:T(8,128)S(1)}, pred[7]{0:T(512)(128)(4,1)}, f32[1,32,1]{1,2,0:T(1,128)S(1)}, f32[7,32,32]{2,1,0:T(8,128)S(1)}...) while((s32[]{:T(128)}, f32[1,32,4096]{2,1,0:T(8,128)S(1)}, pred[7]{0:T(512)(128)(4,1)}, ...), condition=%wide.region_9.10_spmd, body=%wide.region_8.9_spmd.sunk | while | flops 102891520 | bytes 9995538 | solution.py:49
  287.3 85.2 %while.139 = (s32[]{:T(128)}, f32[1,32,4096]{2,1,0:T(8,128)S(1)}, s32[7]{0:T(128)S(1)}, f32[7,32,32]{2,1,0:T(8,128)S(1)}, f32[7,1,32,4096]{3,2,1,0:T(8,128)}, /*...) while((s32[]{:T(128)}, f32[1,32,4096]{2,1,0:T(8,128)S(1)}, ...), condition=%wide.region_11.12_spmd, body=%wide.region_10.11_spmd.sunk | while | flops 102498304 | bytes 8457133 | solution.py:49
  292.1 3.9 fusion.343
  328.6 3.9 fusion.343
  340.8 3.9 fusion.343
  352.9 3.9 fusion.343
  372.5 68.0 %while.135 = (s32[]{:T(128)}, f32[1,32,4096]{2,1,0:T(8,128)S(1)}, s32[]{:T(128)}, f32[32]{0:T(128)S(1)}, f32[8,32,32]{2,1,0:T(8,128)S(1)}, /*index=5*/f32[8,32]{1,0:T(8,128)}, s32[]{:T(128)}) while((s32[]{:T(128)}, f32[1,32,4096]{2,1,0:T(8,128)S(1)}, s32[]{:T(128)}, f32[32]{0:T(128)S(1)}, f32[8,32,32]{2,1,0:T(8,128)S(1)}, ...), condition=%wide.region_3.4_spmd, body=%wide.region_2.3_spmd.sunk | while | flops 102105120 | bytes 6325867 | solution.py:49
  441.5 4.5 fusion.176
  461.3 4.9 fusion.177
  471.3 106.5 %while.140 = (s32[]{:T(128)}, f32[8,32,32]{2,1,0:T(8,128)S(1)}, f32[8,32]{1,0:T(8,128)S(1)}, f32[1,32,4096]{2,1,0:T(8,128)S(1)}, s32[7]{0:T(128)S(1)}, /*index=5...) while((s32[]{:T(128)}, f32[8,32,32]{2,1,0:T(8,128)S(1)}, ...), condition=%wide.region_14.15_spmd, body=%wide.region_12.14_spmd.sunk | while | flops 204081152 | bytes 10050626 | solution.py:49
  581.8 12.1 %all-reduce.24 = (f32[8,32,32]{2,1,0:T(8,128)}, f32[8,32]{1,0:T(8,128)}) all-reduce(f32[8,32,32]{2,1,0:T(8,128)S(1)} %fusion.164, f32[8,32]{1,0:T(8,128)S(1)} %add_any.216), channel_id=1, replica_groups=mesh['depth'=8,'batch'=4] {'batch'}, use_global_device_ids=true, to_apply=%region_15.16 | all-reduce | flops 8448 | bytes 67584 | tf_op jit(solution)/shard_map/psum | solution.py:100
  595.0 46.3 %while.136 = (s32[]{:T(128)}, f32[1,32,4096]{2,1,0:T(8,128)S(1)}, f32[8,1,32,4096]{3,2,1,0:T(8,128)}, s32[8]{0:T(128)S(1)}, f32[32]{0:T(128)S(1)}, /*index=5*/f3...) while((s32[]{:T(128)}, f32[1,32,4096]{2,1,0:T(8,128)S(1)}, ...), condition=%wide.region_5.6_spmd, body=%wide.region_4.5_spmd.sunk | while | flops 102105120 | bytes 7899809 | solution.py:81
  (536 shorter events, 501.7 us)
Async XLA Ops:
  7.2 586.7 %all-gather.6.cloned.1.call-start = ((), (), s32[]{:S(2)}) async-start(), calls=%async_computation | async-start | bytes 4718592 | tf_op jit(solution)/shard_map/all_gather | solution.py:71
  10.8 3.4 copy-start.11
  15.8 3.4 copy-start.11
  20.7 3.4 copy-start.11
  25.7 3.4 copy-start.11
  30.7 3.4 copy-start.11
  35.6 3.4 copy-start.11
  40.6 3.4 copy-start.11
  45.6 5.1 copy-start.12
  45.6 5.1 copy-start.8
  47.5 11.3 %copy-start.5 = (f32[1,1,32,4096]{3,2,1,0:T(8,128)S(1)}, f32[1,1,32,4096]{3,2,1,0:T(8,128)}, u32[]{:S(2)}) copy-start(f32[1,1,32,4096]{3,2,1,0:T(8,128)} %param.21) | copy-start | bytes 1572868
  53.1 61.6 %collective-permute-start = (f32[1,32,4096]{2,1,0:T(8,128)}, f32[1,32,4096]{2,1,0:T(8,128)}, u32[]{:S(2)}, u32[]{:S(2)}) collective-permute-start(f32[1,32,4096]{2,1,0:T(8,128)} %fusion.161), channel_id=1, source_target_pairs={{0,4},{4,8},{8,12},{12,16},{16,20},{20,24},{24,28},{1,5},{5,9},{9,... | collective-permute-start | bytes 1572872 | tf_op jit(solution)/shard_map/ppermute | solution.py:14
  58.8 56.0 %copy-start.10 = (f32[1,1,32,4096]{3,2,1,0:T(8,128)S(1)}, f32[1,1,32,4096]{3,2,1,0:T(8,128)}, u32[]{:S(2)}) copy-start(f32[1,1,32,4096]{3,2,1,0:T(8,128)} %param.20) | copy-start | bytes 1572868
  115.6 5.1 copy-start.2
  115.7 479.3 %all-gather.8.cloned.1.call-start = ((), (), s32[]{:S(2)}) async-start(), calls=%async_computation.1 | async-start | bytes 4718592 | tf_op jit(solution)/shard_map/all_gather | solution.py:72
  215.4 3.2 copy-start.1
  278.6 177.0 %collective-permute-start.1 = (f32[1,32,4096]{2,1,0:T(8,128)S(1)}, f32[1,32,4096]{2,1,0:T(8,128)}, u32[]{:S(2)}, u32[]{:S(2)}) collective-permute-start(f32[1,32,4096]{2,1,0:T(8,128)S(1)} %get-tuple-element.1245), channel_id=1, source_target_pairs={{4,0},{8,4},{12,8},{16,12},{20,16},{24,20},{28,24},{5,1},{9,5},{13... | collective-permute-start | bytes 1572872 | tf_op jit(solution)/shard_map/ppermute | solution.py:14
  446.0 7.8 %copy-start.3 = (f32[1,32,4096]{2,1,0:T(8,128)S(1)}, f32[1,32,4096]{2,1,0:T(8,128)}, u32[]{:S(2)}) copy-start(f32[1,32,4096]{2,1,0:T(8,128)} %broadcast_select_fusion) | copy-start | bytes 1572868
  447.6 8.0 %copy-start.6 = (f32[1,1,32,4096]{3,2,1,0:T(8,128)S(1)}, f32[1,1,32,4096]{3,2,1,0:T(8,128)}, u32[]{:S(2)}) copy-start(f32[1,1,32,4096]{3,2,1,0:T(8,128)} %param.21) | copy-start | bytes 1572868
  455.6 12.9 %copy-start.4 = (f32[4096,32]{0,1:T(8,128)}, f32[4096,32]{0,1:T(8,128)S(1)}, u32[]{:S(2)}) copy-start(f32[4096,32]{0,1:T(8,128)S(1)} %fusion.189) | copy-start | bytes 1572868
  458.6 11.5 %copy-start.7 = (f32[1,32,4096]{2,1,0:T(8,128)}, f32[1,32,4096]{2,1,0:T(8,128)S(1)}, u32[]{:S(2)}) copy-start(f32[1,32,4096]{2,1,0:T(8,128)S(1)} %get-tuple-element.1391) | copy-start | bytes 1572868
  466.2 5.1 copy-start.14
  577.8 17.2 %copy-start = (f32[1,32,4096]{2,1,0:T(8,128)}, f32[1,32,4096]{2,1,0:T(8,128)S(1)}, u32[]{:S(2)}) copy-start(f32[1,32,4096]{2,1,0:T(8,128)S(1)} %get-tuple-element.1253) | copy-start | bytes 1572868
  577.8 17.2 %copy-start.13 = (s32[8]{0:T(128)S(1)}, s32[8]{0:T(128)}, u32[]{:S(2)}) copy-start(s32[8]{0:T(128)} %param.25) | copy-start | bytes 100
  (7 other events, 22.3 us)
Sparse Core Ops, SparseCore 0:
  115.8 71.7 all-gather.5
  470.3 74.7 all-gather.7
where the time goes:
time: 663 us; the launch traced here: 650 us
  matrix products  214 us (32%)
  local copies, waits for them, and re-layouts  192 us (29%)
  other arithmetic  146 us (22%)
  blocking collectives  65.7 us (10%)
  between operations  16.7 us (3%)
  loops' own time  7.83 us (1%)
  starting transfers between devices  7.72 us (1%)
    dot_general x63, matrix products, apply_layer(): jnp.einsum('ji,bjp->bip', matrix, jnp.tanh(pre_act), precision=lax.Precis...  124 us
    sub x39, other arithmetic, laplace(): return (beside_all - 4.0 * shaped).reshape(states.shape)  98.4 us
    dot_general x65, matrix products, apply_layer(): jnp.einsum('ij,bjp->bip', matrix, states, precision=lax.Precision.HIGHEST)  90 us
    reshape x55, local copies, waits for them, and re-layouts, laplace(): shaped = states.reshape(states.shape[:-1] + (IMG_H, IMG_W))  65.1 us
    reshape x54, local copies, waits for them, and re-layouts, laplace(): return (beside_all - 4.0 * shaped).reshape(states.shape)  32.4 us
    all_gather x1, blocking collectives, body(): lax.all_gather(weights[:1], 'depth', axis=0, tiled=True)  30.5 us
    add_any x16, other arithmetic, laplace(): padded = jnp.pad(shaped, [(0, 0)] * (shaped.ndim - 2) + [(1, 1), (1, 1)])  28.2 us
    dynamic_update_slice x42, local copies, waits for them, and re-layouts, section(): relaxed = lax.fori_loop(0, MOST - 1, advance, states)  23.4 us
  transfers between devices with their start and end apart: 4, of which 0 were waited for; matrix products, arithmetic and copies ran while one was open for 72% of the time, Pallas kernels for 0%

commit v1 on v0

v1 whole, which is shorter than its diff:
```python
import functools

import jax
import jax.numpy as jnp
from jax import lax
from jax.experimental import pallas as pl
from jax.experimental.pallas import tpu as pltpu
from jax.sharding import PartitionSpec as P

IMG = 64
LANES = 128
CHUNK = 512
F32 = jnp.float32
BF16 = jnp.bfloat16


def split(x):
    hi = x.astype(BF16)
    lo = (x - hi.astype(F32)).astype(BF16)
    return hi, lo


def stack3(hi, lo):
    return jnp.concatenate([hi, lo, hi], axis=0)


def left_factor(matrix):
    hi = matrix.astype(BF16).astype(F32)
    return jnp.concatenate([hi, hi, matrix - hi], axis=1).astype(BF16)


def mm(a, b):
    return jnp.dot(a, b, preferred_element_type=F32)


def mm_nt(a, b):
    return lax.dot_general(a, b, (((1,), (1,)), ((), ())), preferred_element_type=F32)


def lane_masks(rows):
    lane = lax.broadcasted_iota(jnp.int32, (rows, LANES), 1)
    col = lane % IMG
    return col > 0, col < IMG - 1, lane < IMG


def neighbours(left, mid, right, masks):
    not_first, not_last, upper = masks
    pieces = [left] + [mid[:, k : k + LANES] for k in range(0, mid.shape[1], LANES)] + [right]
    swapped = [pltpu.roll(piece, IMG, 1) for piece in pieces]
    sums = []
    for k in range(1, len(pieces) - 1):
        piece = pieces[k]
        beside = jnp.where(not_first, pltpu.roll(piece, 1, 1), 0.0)
        beside += jnp.where(not_last, pltpu.roll(piece, LANES - 1, 1), 0.0)
        beside += swapped[k] + jnp.where(upper, swapped[k - 1], swapped[k + 1])
        sums.append(beside)
    return jnp.concatenate(sums, axis=1)


def sweep(buf, width, step):
    rows = buf.shape[0]
    masks = lane_masks(rows)
    before = buf[:, 0:LANES]
    for start in range(0, width, CHUNK):
        size = min(CHUNK, width - start)
        at = LANES + start
        mid = buf[:, at : at + size]
        after = buf[:, at + size : at + size + LANES]
        around = neighbours(before, mid, after, masks)
        before = mid[:, size - LANES :]
        buf[:, at : at + size] = step(start, size, mid, around)


def prepare(w_ref, wl_ref, wt_ref, factor):
    for slot in range(w_ref.shape[0]):
        matrix = w_ref[slot]
        wl_ref[slot] = left_factor(matrix)
        wt_ref[slot] = left_factor((factor * matrix).T)


def bias_of(bt_ref, slot):
    table = bt_ref[...]
    pick = lax.broadcasted_iota(jnp.int32, table.shape, 1) == slot
    return jnp.sum(jnp.where(pick, table, 0.0), axis=1, keepdims=True)


def forward_layer(buf, width, wl, wt, bias, spread, t_out=None, u_out=None):
    keep = 1.0 - 4.0 * spread

    def step(start, size, mid, around):
        hi, lo = split(mid)
        t_hi, t_lo = split(jnp.tanh(mm(wl, stack3(hi, lo)) + bias))
        if t_out is not None:
            t_out(start, size, t_hi, t_lo)
        if u_out is not None:
            u_out(start, size, hi, lo)
        return mid * keep + around * spread - mm(wt, stack3(t_hi, t_lo))

    sweep(buf, width, step)


def run_forward(buf, width, wl_ref, wt_ref, bt_ref, spread, count, t_refs=None, u_refs=None):
    def saver(refs, slot):
        if refs is None:
            return None

        def save(start, size, hi, lo):
            refs[0][slot, :, start : start + size] = hi
            refs[1][slot, :, start : start + size] = lo

        return save

    @pl.loop(0, count)
    def _(slot):
        forward_layer(
            buf, width, wl_ref[slot], wt_ref[slot], bias_of(bt_ref, slot), spread,
            saver(t_refs, slot), saver(u_refs, slot),
        )


def run_backward(buf, width, wl_ref, wt_ref, spread, count, t_refs, u_refs=None, grads=None):
    keep = 1.0 - 4.0 * spread

    @pl.loop(0, count)
    def _(passed):
        slot = count - 1 - passed
        wl, wt = wl_ref[slot], wt_ref[slot]
        rows = buf.shape[0]
        total = [None, None]

        def step(start, size, mid, around):
            hi, lo = split(mid)
            t_hi = t_refs[0][slot, :, start : start + size]
            t_lo = t_refs[1][slot, :, start : start + size]
            t = t_hi.astype(F32) + t_lo.astype(F32)
            q = (1.0 - t * t) * mm(wl, stack3(hi, lo))
            q_hi, q_lo = split(q)
            if grads is not None:
                u_hi = u_refs[0][slot, :, start : start + size]
                u_lo = u_refs[1][slot, :, start : start + size]
                left = jnp.concatenate([t_hi, t_lo, q_hi, q_lo], axis=0)
                right = jnp.concatenate([hi, lo, u_hi, u_lo], axis=0)
                part = mm_nt(left, right)
                part_b = sum(q[:, k : k + LANES] for k in range(0, size, LANES))
                total[0] = part if total[0] is None else total[0] + part
                total[1] = part_b if total[1] is None else total[1] + part_b
            return mid * keep + around * spread - mm(wt, stack3(q_hi, q_lo))

        sweep(buf, width, step)
        if grads is not None:
            gw_ref, gb_ref, factor = grads
            g = total[0]
            a, b, c, d = rows, 2 * rows, 3 * rows, 4 * rows
            gw = g[0:a, 0:a] + g[0:a, a:b] + g[a:b, 0:a]
            gw += g[b:c, b:c] + g[b:c, c:d] + g[c:d, b:c]
            gw_ref[slot] = -factor * gw
            column = jnp.sum(total[1], axis=1, keepdims=True)
            pick = lax.broadcasted_iota(jnp.int32, gb_ref.shape, 1) == slot
            gb_ref[...] = jnp.where(pick, -factor * column, gb_ref[...])


def fill(buf, value):
    rows, width = value.shape
    zero = jnp.zeros((rows, LANES), F32)
    buf[:, 0:LANES] = zero
    buf[:, LANES + width :] = zero
    buf[:, LANES : LANES + width] = value


def inner(buf):
    return buf[:, LANES : buf.shape[1] - LANES]


def push_kernel(len_ref, guess_ref, w_ref, bt_ref, diff_ref, out_ref, buf, wl, wt):
    most = w_ref.shape[0]
    factor = 1.0 / most
    own = lax.axis_index("depth")
    prepare(w_ref, wl, wt, factor)
    fill(buf, guess_ref[...])
    run_forward(buf, guess_ref.shape[1], wl, wt, bt_ref, factor * diff_ref[...], len_ref[own])
    out_ref[...] = inner(buf)


def tau_kernel(len_ref, point_ref, w_ref, bt_ref, diff_ref, out_ref, buf, wl, wt):
    most = w_ref.shape[0]
    factor = 1.0 / most
    own = lax.axis_index("depth")
    count = len_ref[jnp.minimum(own + 1, lax.axis_size("depth") - 1)]
    width = point_ref.shape[1]
    prepare(w_ref, wl, wt, factor)
    point = point_ref[...]
    fill(buf, point)
    run_forward(buf, width, wl, wt, bt_ref, factor * diff_ref[...], count)
    out_ref[...] = inner(buf)

    @pl.when(own > 0)
    def _():
        coarse_factor = count.astype(F32) * factor
        buf[:, LANES : LANES + width] = point_ref[...]
        forward_layer(
            buf, width, wl[0], left_factor((coarse_factor * w_ref[0]).T), bias_of(bt_ref, 0),
            coarse_factor * diff_ref[...],
        )
        out_ref[...] = out_ref[...] - inner(buf)


def adjoint_kernel(
    len_ref, guess_ref, before_ref, after_ref, adj_ref, adj_after_ref,
    w_ref, bt_ref, w_before_ref, bt_before_ref, w_after_ref, bt_after_ref, diff_ref,
    point_ref, adj_out_ref, gw_ref, gb_ref,
    buf, wl, wt, t_hi, t_lo, u_hi, u_lo,
):
    most = w_ref.shape[0]
    factor = 1.0 / most
    own = lax.axis_index("depth")
    last = lax.axis_size("depth") - 1
    width = guess_ref.shape[1]
    spread = factor * diff_ref[...]
    gw_ref[...] = jnp.zeros_like(gw_ref)
    gb_ref[...] = jnp.zeros_like(gb_ref)

    @pl.when(own < last)
    def _():
        count = len_ref[jnp.minimum(own + 1, last)]
        prepare(w_after_ref, wl, wt, factor)
        fill(buf, after_ref[...])
        run_forward(buf, width, wl, wt, bt_after_ref, spread, count, (t_hi, t_lo))
        fill(buf, adj_after_ref[...])
        run_backward(buf, width, wl, wt, spread, count, (t_hi, t_lo))
        adj_out_ref[...] = inner(buf)

    @pl.when(own == last)
    def _():
        adj_out_ref[...] = adj_ref[...]

    @pl.when(own > 0)
    def _():
        count = len_ref[jnp.maximum(own - 1, 0)]
        prepare(w_before_ref, wl, wt, factor)
        fill(buf, before_ref[...])
        run_forward(buf, width, wl, wt, bt_before_ref, spread, count)
        point_ref[...] = inner(buf)

    @pl.when(own == 0)
    def _():
        point_ref[...] = guess_ref[...]

    count = len_ref[own]
    prepare(w_ref, wl, wt, factor)
    fill(buf, point_ref[...])
    run_forward(buf, width, wl, wt, bt_ref, spread, count, (t_hi, t_lo), (u_hi, u_lo))
    fill(buf, adj_out_ref[...])
    run_backward(
        buf, width, wl, wt, spread, count, (t_hi, t_lo), (u_hi, u_lo), (gw_ref, gb_ref, factor)
    )
    adj_out_ref[...] = inner(buf)


def chain_kernel(sources, most, len_ref, point_ref, w0_ref, bt0_ref, diff_ref, *rest):
    items = rest[: len(sources)]
    out_ref, buf, held, sem = rest[len(sources) :]
    own = lax.axis_index("depth")
    count = held.shape[0]
    width = point_ref.shape[1]
    copies = [
        pltpu.make_async_copy(item, held.at[source(own)], sem.at[k])
        for k, (item, source) in enumerate(zip(items, sources))
    ]
    for copy in copies:
        copy.start()
    for copy in copies:
        copy.wait()
    fill(buf, held[0])

    @pl.loop(2, own)
    def _(section):
        factor = len_ref[section].astype(F32) * (1.0 / most)
        entry = lax.rem(section - own + count, count)
        matrix = w0_ref[entry]
        forward_layer(
            buf, width, left_factor(matrix), left_factor((factor * matrix).T),
            bias_of(bt0_ref, entry), factor * diff_ref[...],
        )
        buf[:, LANES : LANES + width] = inner(buf) + held[section - 1]

    @pl.when(own < 2)
    def _():
        out_ref[...] = point_ref[...]

    @pl.when(own >= 2)
    def _():
        out_ref[...] = inner(buf)


SMEM = pl.BlockSpec(memory_space=pltpu.SMEM)
VMEM = pl.BlockSpec(memory_space=pltpu.VMEM)
ANY = pl.BlockSpec(memory_space=pl.ANY)


def call(kernel, out_shape, in_specs, scratch, flops, name):
    return pl.pallas_call(
        kernel,
        out_shape=out_shape,
        in_specs=in_specs,
        out_specs=jax.tree.map(lambda _: VMEM, out_shape),
        scratch_shapes=scratch,
        compiler_params=pltpu.CompilerParams(vmem_limit_bytes=48 * 2**20),
        cost_estimate=pl.CostEstimate(flops=flops, bytes_accessed=2**21, transcendentals=0),
        name=name,
    )


def shifted(value, steps):
    count = lax.axis_size("depth")
    first, end = max(0, -steps), min(count, count - steps)
    return lax.ppermute(value, "depth", [(s, s + steps) for s in range(first, end)])


def gather_small(value):
    count = lax.axis_size("depth")
    have, held = 1, value[None]
    while have < count:
        take = min(have, count - have)
        more = lax.ppermute(held[:take], "depth", [((s + have) % count, s) for s in range(count)])
        held = jnp.concatenate([held, more], axis=0)
        have += take
    return held


def batch_sum(values):
    count = lax.axis_size("batch")
    if count & (count - 1):
        return lax.psum(values, "batch")
    gap = 1
    while gap < count:
        pairs = [(s, s ^ gap) for s in range(count)]
        values = jax.tree.map(lambda v: v + lax.ppermute(v, "batch", pairs), values)
        gap *= 2
    return values


def body(cpoint_guess, adjoint_guess, weights, biases, diffusion, section_len):
    count = lax.axis_size("depth")
    most, rows, _ = weights.shape
    width = cpoint_guess.shape[-1]
    guess, adjoint = cpoint_guess[0, 0], adjoint_guess[0, 0]
    diff = diffusion[:, None]
    state = jax.ShapeDtypeStruct((rows, width), F32)
    buffer = pltpu.VMEM((rows, width + 2 * LANES), F32)
    factors = [pltpu.VMEM((most, rows, 3 * rows), BF16)] * 2

    packed = jnp.concatenate([weights, biases[:, None, :]], axis=1)
    packed_after = shifted(packed, -1)
    packed_before = shifted(packed, 1)
    adj_after = shifted(adjoint, -1)
    before = shifted(guess, 1)
    packed0 = gather_small(packed[0])

    def parts(array):
        return array[:, :rows, :], array[:, rows, :].T

    w_after, bt_after = parts(packed_after)
    w_before, bt_before = parts(packed_before)
    w_zero, bt_zero = parts(packed0)
    bt = biases.T

    layer = 16 * rows * rows * width
    after = call(push_kernel, state, [SMEM, VMEM, VMEM, VMEM, VMEM], [buffer, *factors], 4 * layer, "push")(
        section_len, guess, weights, bt, diff
    )
    item = call(tau_kernel, state, [SMEM, VMEM, VMEM, VMEM, VMEM], [buffer, *factors], 4 * layer, "tau")(
        section_len, after, w_after, bt_after, diff
    )

    ring = list(range(0, count, 2)) + list(range(1, count, 2))[::-1]
    place = {device: k for k, device in enumerate(ring)}
    forth = [(ring[k], ring[(k + 1) % count]) for k in range(count)]
    back = [(b, a) for a, b in forth]

    def source(shift):
        table = [ring[(place[d] - shift) % count] for d in range(count)]

        def at(own):
            found = jnp.int32(0)
            for d in range(count):
                found = jnp.where(own == d, table[d], found)
            return found

        return at

    items, sources = [item], [source(0)]
    ahead = behind = item
    for k in range(1, count // 2 + 1):
        ahead = lax.ppermute(ahead, "depth", forth)
        items.append(ahead)
        sources.append(source(k))
        if 2 * k < count:
            behind = lax.ppermute(behind, "depth", back)
            items.append(behind)
            sources.append(source(-k))

    saved = [pltpu.VMEM((most, rows, width), BF16)] * 4
    point, adjoint_out, gw, gbt = call(
        adjoint_kernel,
        [state, state, jax.ShapeDtypeStruct(weights.shape, F32), jax.ShapeDtypeStruct((rows, most), F32)],
        [SMEM] + [VMEM] * 12, [buffer, *factors, *saved], 20 * layer, "adjoint",
    )(
        section_len, guess, before, after, adjoint, adj_after,
        weights, bt, w_before, bt_before, w_after, bt_after, diff,
    )
    gw, gbt = batch_sum((gw, gbt))

    states = call(
        functools.partial(chain_kernel, sources, most), state,
        [SMEM, VMEM, VMEM, VMEM, VMEM] + [ANY] * count,
        [buffer, pltpu.VMEM((count, rows, width), F32), pltpu.SemaphoreType.DMA((count,))],
        4 * layer, "chain",
    )(section_len, point, w_zero, bt_zero, diff, *items)
    return states[None, None], adjoint_out[None, None], gw, gbt.T


def solution(mesh):
    state = P("depth", "batch", None, None)
    return jax.shard_map(
        body,
        mesh=mesh,
        in_specs=(state, state, P("depth", None, None), P("depth", None), P(), P()),
        out_specs=(state, state, P("depth", None, None), P("depth", None)),
        check_vma=False,
    )
```

time: 663 us -> 152 us (0.23)
  the two profiles are of different devices: /device:TPU:0 before, /device:TPU:8 now
where the time goes in v1:
time: 152 us
  Pallas kernels  56.1 us (37%)
  waiting for transfers between devices  53.9 us (35%)
  starting transfers between devices  23.8 us (16%)
  local copies, waits for them, and re-layouts  14.4 us (9%)
  other arithmetic  2.36 us (2%)
    pallas_call x1, Pallas kernels, body(): call(adjoint_kernel, [state, state, jax.ShapeDtypeStruct(weights.shape, F...  35.7 us
    ppermute x3, waiting for transfers between devices, gather_small(): lax.ppermute(held[:take], 'depth', [((s + have) % count, s) for s in rang...  22.7 us
    ppermute x4, waiting for transfers between devices, body(): ahead = lax.ppermute(ahead, 'depth', forth)  21.8 us
    pallas_call x1, Pallas kernels, body(): call(tau_kernel, state, [SMEM, VMEM, VMEM, VMEM, VMEM], [buffer, *factors...  13.6 us
    unnamed x59, local copies, waits for them, and re-layouts  12.6 us
    ppermute x4, starting transfers between devices, shifted(): lax.ppermute(value, 'depth', [(s, s + steps) for s in range(first, end)])  12 us
    ppermute x4, waiting for transfers between devices, batch_sum(): values = jax.tree.map(lambda v: v + lax.ppermute(v, 'batch', pairs), values)  4.78 us
    ppermute x4, waiting for transfers between devices, shifted(): lax.ppermute(value, 'depth', [(s, s + steps) for s in range(first, end)])  4.58 us
  transfers between devices with their start and end apart: 18, of which 8 were waited for; matrix products, arithmetic and copies ran while one was open for 5% of the time, Pallas kernels for 26%

profile of v1, /device:TPU:8, one launch (start us, length us, event | category | flops | bytes accessed | tf_op | source)
XLA Modules:
  0.0 151.6 jit_solution(4382659476872012583)
XLA Ops:
  0.6 1.1 copy.37
  1.7 0.8 copy.38
  3.2 3.3 %collective-permute-start.3 = (f32[8,33,32]{1,2,0:T(8,128)S(1)}, f32[8,33,32]{1,2,0:T(8,128)S(1)}, u32[]{:S(2)}, u32[]{:S(2)}) collective-permute-start(f32[8,33,32]{1,2,0:T(8,128)S(1)} %pad_maximum_fusion.1), channel_id=1, source_target_pairs={{4,0},{8,4},{12,8},{16,12},{20,16},{24,20},{28,24},{5,1},{9,5},{13... | collective-permute-start | bytes 101384 | tf_op jit(solution)/shard_map/ppermute | solution.py:316
  8.0 3.6 %push.1.after_ref.point_ref = f32[32,4096]{1,0:T(8,128)S(1)} custom-call(s32[8]{0:T(128)S(1)} %copy-done.10, f32[32,4096]{1,0:T(8,128)S(1)} %bitcast.21, f32[8,32,32]{2,1,0:T(8,128)S(1)} %copy-done, f32[32,8]{1,0:T(8,128)S(1)} %bitcast.27, f32[32,1]{1,0:T(8,128)S(1)} %copy.36.diff_ref), custom_call_target="tpu_custom_call" | custom-call | flops 268435456 | bytes 2097152 | tf_op jit(solution)/shard_map/push/pallas_call | solution.py:368
  12.6 13.6 %tau.1.rest_0_ = f32[32,4096]{1,0:T(8,128)S(1)} custom-call(s32[8]{0:T(128)S(1)} %copy-done.10, f32[32,4096]{1,0:T(8,128)S(1)} %push.1.after_ref.point_ref, f32[8,32,32]{2,1,0:T(8,128)S(1)} %copy.51.w_after_ref.w_ref, f32[32,8]{1,0:T(8,128)S(1)} %bitcast.24, f32[32,1]{1,0:T(8,128)S(1)} %copy.36.diff_ref), custom_call_target="tpu_custom_call" | custom-call | flops 268435456 | bytes 2097152 | tf_op jit(solution)/shard_map/tau/pallas_call | solution.py:371
  26.3 2.0 %collective-permute-start.8 = (f32[32,4096]{1,0:T(8,128)S(1)}, f32[32,4096]{1,0:T(8,128)S(1)}, u32[]{:S(2)}, u32[]{:S(2)}) collective-permute-start(f32[32,4096]{1,0:T(8,128)S(1)} %tau.1.rest_0_), channel_id=1, source_target_pairs={{8,0},{16,8},{24,16},{28,24},{20,28},{12,20},{4,12},{0,4},{9,1},{1... | collective-permute-start | bytes 1572872 | tf_op jit(solution)/shard_map/ppermute | solution.py:398
  28.3 11.4 %collective-permute-done.7.rest_1_ = f32[32,4096]{1,0:T(8,128)S(1)} collective-permute-done((f32[32,4096]{1,0:T(8,128)S(1)}, f32[32,4096]{1,0:T(8,128)S(1)}, u32[]{:S(2)}, u32[]{:S(2)}) %collective-permute-start.7) | collective-permute-done | bytes 524320 | tf_op jit(solution)/shard_map/ppermute | solution.py:394
  40.0 1.7 %collective-permute-start.10 = (f32[32,4096]{1,0:T(8,128)S(1)}, f32[32,4096]{1,0:T(8,128)}, u32[]{:S(2)}, u32[]{:S(2)}) collective-permute-start(f32[32,4096]{1,0:T(8,128)S(1)} %collective-permute-done.8.rest_2_), channel_id=1, source_target_pairs={{8,0},{16,8},{24,16},{28,24},{20,28},{12,20},{4,12},{0,4},{9,1},{1... | collective-permute-start | bytes 1572872 | tf_op jit(solution)/shard_map/ppermute | solution.py:398
  41.7 10.4 %collective-permute-done.9.rest_3_ = f32[32,4096]{1,0:T(8,128)S(1)} collective-permute-done((f32[32,4096]{1,0:T(8,128)S(1)}, f32[32,4096]{1,0:T(8,128)S(1)}, u32[]{:S(2)}, u32[]{:S(2)}) %collective-permute-start.9) | collective-permute-done | bytes 524320 | tf_op jit(solution)/shard_map/ppermute | solution.py:394
  52.8 2.5 %collective-permute-start = (f32[32,4096]{1,0:T(8,128)S(1)}, f32[32,4096]{1,0:T(8,128)}, u32[]{:S(2)}, u32[]{:S(2)}) collective-permute-start(f32[32,4096]{1,0:T(8,128)S(1)} %bitcast.22), channel_id=1, source_target_pairs={{0,4},{4,8},{8,12},{12,16},{16,20},{20,24},{24,28},{1,5},{5,9},{9,... | collective-permute-start | bytes 1572872 | tf_op jit(solution)/shard_map/ppermute | solution.py:316
  55.3 4.3 %collective-permute-start.1 = (f32[32,4096]{1,0:T(8,128)}, f32[32,4096]{1,0:T(8,128)}, u32[]{:S(2)}, u32[]{:S(2)}) collective-permute-start(f32[32,4096]{1,0:T(8,128)} %bitcast.3.adj_ref), channel_id=1, source_target_pairs={{4,0},{8,4},{12,8},{16,12},{20,16},{24,20},{28,24},{5,1},{9,5},{13... | collective-permute-start | bytes 1572872 | tf_op jit(solution)/shard_map/ppermute | solution.py:316
  60.0 18.8 %collective-permute-done.4 = f32[1,33,32]{1,2,0:T(8,128)S(1)} collective-permute-done((f32[1,33,32]{1,2,0:T(8,128)S(1)}, f32[1,33,32]{1,2,0:T(8,128)S(1)}, u32[]{:S(2)}, u32[]{:S(2)}) %collective-permute-start.4) | collective-permute-done | bytes 4256 | tf_op jit(solution)/shard_map/ppermute | solution.py:324
  78.9 3.9 %collective-permute-done.5 = f32[2,33,32]{1,2,0:T(8,128)S(1)} collective-permute-done((f32[2,33,32]{1,2,0:T(8,128)S(1)}, f32[2,33,32]{1,2,0:T(8,128)S(1)}, u32[]{:S(2)}, u32[]{:S(2)}) %collective-permute-start.5) | collective-permute-done | bytes 8480 | tf_op jit(solution)/shard_map/ppermute | solution.py:324
  82.8 1.9 %collective-permute-start.2 = (f32[8,33,32]{1,2,0:T(8,128)S(1)}, f32[8,33,32]{1,2,0:T(8,128)S(1)}, u32[]{:S(2)}, u32[]{:S(2)}) collective-permute-start(f32[8,33,32]{1,2,0:T(8,128)S(1)} %copy-done.20), channel_id=1, source_target_pairs={{0,4},{4,8},{8,12},{12,16},{16,20},{20,24},{24,28},{1,5},{5,9},{9,... | collective-permute-start | bytes 101384 | tf_op jit(solution)/shard_map/ppermute | solution.py:316
  84.8 2.0 %collective-permute-start.13 = (f32[32,4096]{1,0:T(8,128)}, f32[32,4096]{1,0:T(8,128)}, u32[]{:S(2)}, u32[]{:S(2)}) collective-permute-start(f32[32,4096]{1,0:T(8,128)} %collective-permute-done.11.rest_5_), channel_id=1, source_target_pairs={{0,8},{8,16},{16,24},{24,28},{28,20},{20,12},{12,4},{4,0},{1,9},{9... | collective-permute-start | bytes 1572872 | tf_op jit(solution)/shard_map/ppermute | solution.py:394
  87.4 4.6 %collective-permute-done.2 = f32[8,33,32]{1,2,0:T(8,128)S(1)} collective-permute-done((f32[8,33,32]{1,2,0:T(8,128)S(1)}, f32[8,33,32]{1,2,0:T(8,128)S(1)}, u32[]{:S(2)}, u32[]{:S(2)}) %collective-permute-start.2) | collective-permute-done | bytes 33824 | tf_op jit(solution)/shard_map/ppermute | solution.py:316
  92.0 2.1 %collective-permute-start.6 = (f32[4,33,32]{1,2,0:T(8,128)}, f32[4,33,32]{1,2,0:T(8,128)}, u32[]{:S(2)}, u32[]{:S(2)}) collective-permute-start(f32[4,33,32]{1,2,0:T(8,128)} %pad_maximum_fusion.2), channel_id=1, source_target_pairs={{16,0},{20,4},{24,8},{28,12},{0,16},{4,20},{8,24},{12,28},{17,1},{... | collective-permute-start | bytes 50696 | tf_op jit(solution)/shard_map/ppermute | solution.py:324
  94.9 1.8 %copy.50 = f32[8,1,32]{0,2,1:T(8,128)} copy(f32[8,1,32]{1,2,0:T(8,128)} %slice.29) | data formatting | bytes 2048
  98.0 0.9 copy-done.4
  101.1 35.7 %adjoint.1 = (f32[32,4096]{1,0:T(8,128)S(1)}, f32[32,4096]{1,0:T(8,128)}, f32[8,32,32]{2,1,0:T(8,128)S(1)}, f32[32,8]{1,0:T(8,128)S(1)}) custom-call(s32[8]{0:T(128)S(1)} %copy-done.11, f32[32,4096]{1,0:T(8,128)S(1)} %bitcast.23, f32[32,4096]{1,0:T(8,128)} %collective-permute-done.before_ref, f32[32,4096]{1,0:T(8,128)S(1)} %push.1.after_ref.point_ref, ...), custom_call_target="tpu_custom_call" | custom-call | flops 1342177280 | bytes 2097152 | tf_op jit(solution)/shard_map/adjoint/pallas_call | solution.py:403
  138.8 1.5 %collective-permute-start.17 = (f32[32,8]{1,0:T(8,128)S(1)}, f32[32,8]{1,0:T(8,128)S(1)}, u32[]{:S(2)}, u32[]{:S(2)}) collective-permute-start(f32[32,8]{1,0:T(8,128)S(1)} %add.14), channel_id=1, source_target_pairs={{0,2},{1,3},{2,0},{3,1},{4,6},{5,7},{6,4},{7,5},{8,10},{9,11},{10,... | collective-permute-start | bytes 3080 | tf_op jit(solution)/shard_map/ppermute | solution.py:337
  140.3 0.9 pad_maximum_fusion
  143.2 3.9 %collective-permute-done.15 = f32[8,32,32]{2,1,0:T(8,128)S(1)} collective-permute-done((f32[8,32,32]{2,1,0:T(8,128)S(1)}, f32[8,32,32]{2,1,0:T(8,128)S(1)}, u32[]{:S(2)}, u32[]{:S(2)}) %collective-permute-start.15) | collective-permute-done | bytes 32800 | tf_op jit(solution)/shard_map/ppermute | solution.py:337
  148.4 3.2 %chain.1 = f32[32,4096]{1,0:T(8,128)} custom-call(s32[8]{0:T(128)S(1)} %copy-done.12, f32[32,4096]{1,0:T(8,128)S(1)} %copy-done.3, f32[8,32,32]{2,1,0:T(8,128)S(1)} %copy.53.w0_ref, f32[32,8]{1,0:T(8,128)S(1)} %bitcast.26, f32[32,1]{1,0:T(8,128)S(1)} %copy.36.diff_ref, f32[32,4096]{1,0:T(8,128)S(1)} %tau.1.rest_0_, ...), custom_call_target="tpu_custom_call" | custom-call | flops 268435456 | bytes 2097152 | tf_op jit(solution)/shard_map/chain/pallas_call | solution.py:413
  (89 shorter events, 14.8 us)
Async XLA Ops:
  3.2 8.4 %copy-start.19 = (f32[8,33,32]{1,2,0:T(8,128)}, f32[8,33,32]{1,2,0:T(8,128)S(1)}, u32[]{:S(2)}) copy-start(f32[8,33,32]{1,2,0:T(8,128)S(1)} %pad_maximum_fusion.1) | copy-start | bytes 101380
  3.2 8.4 %collective-permute-start.3 = (f32[8,33,32]{1,2,0:T(8,128)S(1)}, f32[8,33,32]{1,2,0:T(8,128)S(1)}, u32[]{:S(2)}, u32[]{:S(2)}) collective-permute-start(f32[8,33,32]{1,2,0:T(8,128)S(1)} %pad_maximum_fusion.1), channel_id=1, source_target_pairs={{4,0},{8,4},{12,8},{16,12},{20,16},{24,20},{28,24},{5,1},{9,5},{13... | collective-permute-start | bytes 101384 | tf_op jit(solution)/shard_map/ppermute | solution.py:316
  12.6 47.0 %copy-start.14 = (f32[8,1,32]{1,2,0:T(8,128)S(1)}, f32[8,1,32]{1,2,0:T(8,128)}, u32[]{:S(2)}) copy-start(f32[8,1,32]{1,2,0:T(8,128)} %copy-done.13) | copy-start | bytes 3076
  26.2 13.4 %collective-permute-start.7 = (f32[32,4096]{1,0:T(8,128)S(1)}, f32[32,4096]{1,0:T(8,128)S(1)}, u32[]{:S(2)}, u32[]{:S(2)}) collective-permute-start(f32[32,4096]{1,0:T(8,128)S(1)} %tau.1.rest_0_), channel_id=1, source_target_pairs={{0,8},{8,16},{16,24},{24,28},{28,20},{20,12},{12,4},{4,0},{1,9},{9... | collective-permute-start | bytes 1572872 | tf_op jit(solution)/shard_map/ppermute | solution.py:394
  26.3 13.7 %collective-permute-start.8 = (f32[32,4096]{1,0:T(8,128)S(1)}, f32[32,4096]{1,0:T(8,128)S(1)}, u32[]{:S(2)}, u32[]{:S(2)}) collective-permute-start(f32[32,4096]{1,0:T(8,128)S(1)} %tau.1.rest_0_), channel_id=1, source_target_pairs={{8,0},{16,8},{24,16},{28,24},{20,28},{12,20},{4,12},{0,4},{9,1},{1... | collective-permute-start | bytes 1572872 | tf_op jit(solution)/shard_map/ppermute | solution.py:398
  39.7 12.5 %collective-permute-start.9 = (f32[32,4096]{1,0:T(8,128)S(1)}, f32[32,4096]{1,0:T(8,128)S(1)}, u32[]{:S(2)}, u32[]{:S(2)}) collective-permute-start(f32[32,4096]{1,0:T(8,128)S(1)} %collective-permute-done.7.rest_1_), channel_id=1, source_target_pairs={{0,8},{8,16},{16,24},{24,28},{28,20},{20,12},{12,4},{4,0},{1,9},{9... | collective-permute-start | bytes 1572872 | tf_op jit(solution)/shard_map/ppermute | solution.py:394
  40.0 44.8 %collective-permute-start.10 = (f32[32,4096]{1,0:T(8,128)S(1)}, f32[32,4096]{1,0:T(8,128)}, u32[]{:S(2)}, u32[]{:S(2)}) collective-permute-start(f32[32,4096]{1,0:T(8,128)S(1)} %collective-permute-done.8.rest_2_), channel_id=1, source_target_pairs={{8,0},{16,8},{24,16},{28,24},{20,28},{12,20},{4,12},{0,4},{9,1},{1... | collective-permute-start | bytes 1572872 | tf_op jit(solution)/shard_map/ppermute | solution.py:398
  52.2 32.7 %collective-permute-start.11 = (f32[32,4096]{1,0:T(8,128)S(1)}, f32[32,4096]{1,0:T(8,128)}, u32[]{:S(2)}, u32[]{:S(2)}) collective-permute-start(f32[32,4096]{1,0:T(8,128)S(1)} %collective-permute-done.9.rest_3_), channel_id=1, source_target_pairs={{0,8},{8,16},{16,24},{24,28},{28,20},{20,12},{12,4},{4,0},{1,9},{9... | collective-permute-start | bytes 1572872 | tf_op jit(solution)/shard_map/ppermute | solution.py:394
  52.8 44.6 %collective-permute-start = (f32[32,4096]{1,0:T(8,128)S(1)}, f32[32,4096]{1,0:T(8,128)}, u32[]{:S(2)}, u32[]{:S(2)}) collective-permute-start(f32[32,4096]{1,0:T(8,128)S(1)} %bitcast.22), channel_id=1, source_target_pairs={{0,4},{4,8},{8,12},{12,16},{16,20},{20,24},{24,28},{1,5},{5,9},{9,... | collective-permute-start | bytes 1572872 | tf_op jit(solution)/shard_map/ppermute | solution.py:316
  55.3 27.5 %copy-start.20 = (f32[8,33,32]{1,2,0:T(8,128)S(1)}, f32[8,33,32]{1,2,0:T(8,128)}, u32[]{:S(2)}) copy-start(f32[8,33,32]{1,2,0:T(8,128)} %copy-done.19) | copy-start | bytes 101380
  55.3 42.1 %collective-permute-start.1 = (f32[32,4096]{1,0:T(8,128)}, f32[32,4096]{1,0:T(8,128)}, u32[]{:S(2)}, u32[]{:S(2)}) collective-permute-start(f32[32,4096]{1,0:T(8,128)} %bitcast.3.adj_ref), channel_id=1, source_target_pairs={{4,0},{8,4},{12,8},{16,12},{20,16},{24,20},{28,24},{5,1},{9,5},{13... | collective-permute-start | bytes 1572872 | tf_op jit(solution)/shard_map/ppermute | solution.py:316
  59.7 27.1 %copy-start.15 = (f32[1,33,32]{1,2,0:T(8,128)}, f32[1,33,32]{1,2,0:T(8,128)S(1)}, u32[]{:S(2)}) copy-start(f32[1,33,32]{1,2,0:T(8,128)S(1)} %fusion) | copy-start | bytes 12676
  59.7 19.1 %collective-permute-start.4 = (f32[1,33,32]{1,2,0:T(8,128)S(1)}, f32[1,33,32]{1,2,0:T(8,128)S(1)}, u32[]{:S(2)}, u32[]{:S(2)}) collective-permute-start(f32[1,33,32]{1,2,0:T(8,128)S(1)} %fusion), channel_id=1, source_target_pairs={{4,0},{8,4},{12,8},{16,12},{20,16},{24,20},{28,24},{0,28},{5,1},{9... | collective-permute-start | bytes 12680 | tf_op jit(solution)/shard_map/ppermute | solution.py:324
  78.8 8.0 %copy-start.17 = (f32[1,33,32]{1,2,0:T(8,128)}, f32[1,33,32]{1,2,0:T(8,128)S(1)}, u32[]{:S(2)}) copy-start(f32[1,33,32]{1,2,0:T(8,128)S(1)} %collective-permute-done.4) | copy-start | bytes 12676
  78.8 4.0 %collective-permute-start.5 = (f32[2,33,32]{1,2,0:T(8,128)S(1)}, f32[2,33,32]{1,2,0:T(8,128)S(1)}, u32[]{:S(2)}, u32[]{:S(2)}) collective-permute-start(f32[2,33,32]{1,2,0:T(8,128)S(1)} %pad_maximum_fusion.3), channel_id=1, source_target_pairs={{8,0},{12,4},{16,8},{20,12},{24,16},{28,20},{0,24},{4,28},{9,1},{1... | collective-permute-start | bytes 25352 | tf_op jit(solution)/shard_map/ppermute | solution.py:324
  82.8 9.2 %collective-permute-start.2 = (f32[8,33,32]{1,2,0:T(8,128)S(1)}, f32[8,33,32]{1,2,0:T(8,128)S(1)}, u32[]{:S(2)}, u32[]{:S(2)}) collective-permute-start(f32[8,33,32]{1,2,0:T(8,128)S(1)} %copy-done.20), channel_id=1, source_target_pairs={{0,4},{4,8},{8,12},{12,16},{16,20},{20,24},{24,28},{1,5},{5,9},{9,... | collective-permute-start | bytes 101384 | tf_op jit(solution)/shard_map/ppermute | solution.py:316
  84.7 63.0 %collective-permute-start.12 = (f32[32,4096]{1,0:T(8,128)}, f32[32,4096]{1,0:T(8,128)}, u32[]{:S(2)}, u32[]{:S(2)}) collective-permute-start(f32[32,4096]{1,0:T(8,128)} %collective-permute-done.10.rest_4_), channel_id=1, source_target_pairs={{8,0},{16,8},{24,16},{28,24},{20,28},{12,20},{4,12},{0,4},{9,1},{1... | collective-permute-start | bytes 1572872 | tf_op jit(solution)/shard_map/ppermute | solution.py:398
  84.8 62.9 %collective-permute-start.13 = (f32[32,4096]{1,0:T(8,128)}, f32[32,4096]{1,0:T(8,128)}, u32[]{:S(2)}, u32[]{:S(2)}) collective-permute-start(f32[32,4096]{1,0:T(8,128)} %collective-permute-done.11.rest_5_), channel_id=1, source_target_pairs={{0,8},{8,16},{16,24},{24,28},{28,20},{20,12},{12,4},{4,0},{1,9},{9... | collective-permute-start | bytes 1572872 | tf_op jit(solution)/shard_map/ppermute | solution.py:394
  92.0 48.3 %collective-permute-start.6 = (f32[4,33,32]{1,2,0:T(8,128)}, f32[4,33,32]{1,2,0:T(8,128)}, u32[]{:S(2)}, u32[]{:S(2)}) collective-permute-start(f32[4,33,32]{1,2,0:T(8,128)} %pad_maximum_fusion.2), channel_id=1, source_target_pairs={{16,0},{20,4},{24,8},{28,12},{0,16},{4,20},{8,24},{12,28},{17,1},{... | collective-permute-start | bytes 50696 | tf_op jit(solution)/shard_map/ppermute | solution.py:324
  101.1 39.2 %copy-start.22 = (f32[2,33,32]{1,2,0:T(8,128)S(1)}, f32[2,33,32]{1,2,0:T(8,128)}, u32[]{:S(2)}) copy-start(f32[2,33,32]{1,2,0:T(8,128)} %copy-done.21) | copy-start | bytes 25348
  137.6 1.2 collective-permute-start.16
  137.6 4.1 %collective-permute-start.14 = (f32[8,32,32]{2,1,0:T(8,128)S(1)}, f32[8,32,32]{2,1,0:T(8,128)S(1)}, u32[]{:S(2)}, u32[]{:S(2)}) collective-permute-start(f32[8,32,32]{2,1,0:T(8,128)S(1)} %get-tuple-element.10), channel_id=1, source_target_pairs={{0,1},{1,0},{2,3},{3,2},{4,5},{5,4},{6,7},{7,6},{8,9},{9,8},{10,11... | collective-permute-start | bytes 98312 | tf_op jit(solution)/shard_map/ppermute | solution.py:337
  138.8 3.7 %collective-permute-start.17 = (f32[32,8]{1,0:T(8,128)S(1)}, f32[32,8]{1,0:T(8,128)S(1)}, u32[]{:S(2)}, u32[]{:S(2)}) collective-permute-start(f32[32,8]{1,0:T(8,128)S(1)} %add.14), channel_id=1, source_target_pairs={{0,2},{1,3},{2,0},{3,1},{4,6},{5,7},{6,4},{7,5},{8,10},{9,11},{10,... | collective-permute-start | bytes 3080 | tf_op jit(solution)/shard_map/ppermute | solution.py:337
  141.7 5.4 %collective-permute-start.15 = (f32[8,32,32]{2,1,0:T(8,128)S(1)}, f32[8,32,32]{2,1,0:T(8,128)S(1)}, u32[]{:S(2)}, u32[]{:S(2)}) collective-permute-start(f32[8,32,32]{2,1,0:T(8,128)S(1)} %add.12), channel_id=1, source_target_pairs={{0,2},{1,3},{2,0},{3,1},{4,6},{5,7},{6,4},{7,5},{8,10},{9,11},{10,... | collective-permute-start | bytes 98312 | tf_op jit(solution)/shard_map/ppermute | solution.py:337
  (19 other events, 44.4 us)

commit v2 on v1

v2 whole, which is shorter than its diff:
```python
import functools

import jax
import jax.numpy as jnp
from jax import lax
from jax.experimental import pallas as pl
from jax.experimental.pallas import tpu as pltpu
from jax.sharding import PartitionSpec as P

IMG = 64
LANES = 128
CHUNK = 256
GRAD_CHUNK = 2048
F32 = jnp.float32
BF16 = jnp.bfloat16


def split(x):
    hi = x.astype(BF16)
    lo = (x - hi.astype(F32)).astype(BF16)
    return hi, lo


def stack3(hi, lo):
    return jnp.concatenate([hi, lo, hi], axis=0)


def left_factor(matrix):
    hi = matrix.astype(BF16).astype(F32)
    return jnp.concatenate([hi, hi, matrix - hi], axis=1).astype(BF16)


def mm(a, b):
    return jnp.dot(a, b, preferred_element_type=F32)


def mm_nt(a, b):
    return lax.dot_general(a, b, (((1,), (1,)), ((), ())), preferred_element_type=F32)


def lane_masks(rows):
    lane = lax.broadcasted_iota(jnp.int32, (rows, LANES), 1)
    col = lane % IMG
    return col > 0, col < IMG - 1, lane < IMG


def neighbours(left, mid, right, masks):
    not_first, not_last, upper = masks
    pieces = [left] + [mid[:, k : k + LANES] for k in range(0, mid.shape[1], LANES)] + [right]
    swapped = [pltpu.roll(piece, IMG, 1) for piece in pieces]
    sums = []
    for k in range(1, len(pieces) - 1):
        piece = pieces[k]
        beside = jnp.where(not_first, pltpu.roll(piece, 1, 1), 0.0)
        beside += jnp.where(not_last, pltpu.roll(piece, LANES - 1, 1), 0.0)
        beside += swapped[k] + jnp.where(upper, swapped[k - 1], swapped[k + 1])
        sums.append(beside)
    return jnp.concatenate(sums, axis=1)


def sweep(buf, width, step, chunk=CHUNK):
    rows = buf.shape[0]
    masks = lane_masks(rows)
    before = buf[:, 0:LANES]
    for start in range(0, width, chunk):
        size = min(chunk, width - start)
        at = LANES + start
        mid = buf[:, at : at + size]
        after = buf[:, at + size : at + size + LANES]
        around = neighbours(before, mid, after, masks)
        before = mid[:, size - LANES :]
        buf[:, at : at + size] = step(start, size, mid, around)


def prepare(p_ref, wl_ref, wt_ref, factor):
    rows = p_ref.shape[2]
    for slot in range(p_ref.shape[0]):
        matrix = p_ref[slot, :rows, :]
        wl_ref[slot] = left_factor(matrix)
        wt_ref[slot] = left_factor((factor * matrix).T)


def column(row):
    n = row.shape[1]
    same = lax.broadcasted_iota(jnp.int32, (n, n), 0) == lax.broadcasted_iota(jnp.int32, (n, n), 1)
    return jnp.sum(jnp.where(same, row, 0.0), axis=1, keepdims=True)


def bias_of(p_ref, slot):
    rows = p_ref.shape[2]
    return column(p_ref[slot, rows : rows + 1, :])


def forward_layer(buf, width, wl, wt, bias, spread, t_out=None, u_out=None):
    keep = 1.0 - 4.0 * spread

    def step(start, size, mid, around):
        hi, lo = split(mid)
        t_hi, t_lo = split(jnp.tanh(mm(wl, stack3(hi, lo)) + bias))
        if t_out is not None:
            t_out(start, size, t_hi, t_lo)
        if u_out is not None:
            u_out(start, size, hi, lo)
        return mid * keep + around * spread - mm(wt, stack3(t_hi, t_lo))

    sweep(buf, width, step)


def run_forward(buf, width, p_ref, wl_ref, wt_ref, spread, count, t_refs=None, u_refs=None):
    def saver(refs, slot):
        if refs is None:
            return None

        def save(start, size, hi, lo):
            refs[0][slot, :, start : start + size] = hi
            refs[1][slot, :, start : start + size] = lo

        return save

    @pl.loop(0, count)
    def _(slot):
        forward_layer(
            buf, width, wl_ref[slot], wt_ref[slot], bias_of(p_ref, slot), spread,
            saver(t_refs, slot), saver(u_refs, slot),
        )


def run_backward(buf, width, wl_ref, wt_ref, spread, count, t_refs, u_refs=None, grads=None):
    keep = 1.0 - 4.0 * spread

    @pl.loop(0, count)
    def _(passed):
        slot = count - 1 - passed
        wl, wt = wl_ref[slot], wt_ref[slot]
        rows = buf.shape[0]
        total = [None, None]

        def step(start, size, mid, around):
            hi, lo = split(mid)
            t_hi = t_refs[0][slot, :, start : start + size]
            t_lo = t_refs[1][slot, :, start : start + size]
            t = t_hi.astype(F32) + t_lo.astype(F32)
            q = (1.0 - t * t) * mm(wl, stack3(hi, lo))
            q_hi, q_lo = split(q)
            if grads is not None:
                u_hi = u_refs[0][slot, :, start : start + size]
                u_lo = u_refs[1][slot, :, start : start + size]
                left = jnp.concatenate([t_hi, t_lo, q_hi, q_lo], axis=0)
                right = jnp.concatenate([hi, lo, u_hi, u_lo], axis=0)
                part = mm_nt(left, right)
                part_b = sum(q[:, k : k + LANES] for k in range(0, size, LANES))
                total[0] = part if total[0] is None else total[0] + part
                total[1] = part_b if total[1] is None else total[1] + part_b
            return mid * keep + around * spread - mm(wt, stack3(q_hi, q_lo))

        sweep(buf, width, step, CHUNK if grads is None else GRAD_CHUNK)
        if grads is not None:
            g_ref, factor = grads
            g = total[0]
            a, b, c, d = rows, 2 * rows, 3 * rows, 4 * rows
            gw = g[0:a, 0:a] + g[0:a, a:b] + g[a:b, 0:a]
            gw += g[b:c, b:c] + g[b:c, c:d] + g[c:d, b:c]
            g_ref[slot, :, 0:rows] = -factor * gw
            g_ref[slot, :, rows : rows + 1] = -factor * jnp.sum(total[1], axis=1, keepdims=True)


def fill(buf, value):
    rows, width = value.shape
    zero = jnp.zeros((rows, LANES), F32)
    buf[:, 0:LANES] = zero
    buf[:, LANES + width :] = zero
    buf[:, LANES : LANES + width] = value


def inner(buf):
    return buf[:, LANES : buf.shape[1] - LANES]


class Plan:
    def __init__(self, count):
        self.count = count
        self.items = count - 2
        self.hosts = count // 2
        self.first = count // 4
        self.block = IMG // self.hosts
        self.rows = min(IMG, self.block + 2 * (count - 4))
        self.rows += self.rows % 2
        self.results = count - 3
        self.local = (self.first - 3) % self.results

    def window(self, host):
        start = host * self.block - (self.count - 4)
        return jnp.clip(start - start % 2, 0, IMG - self.rows)

    def in_pairs(self, shift):
        return [((h + shift) % self.items, h + self.first) for h in range(self.hosts)]

    def out_pairs(self, shift):
        pairs = [(h + self.first, 3 + (h + shift) % self.results) for h in range(self.hosts)]
        pairs = [(s, d) for s, d in pairs if s != d]
        return pairs + ([(0, 2)] if shift < self.hosts else [])


def lanes(row, size):
    return pl.ds(pl.multiple_of(row * IMG, LANES), size * IMG)


def push_kernel(len_ref, guess_ref, p_ref, diff_ref, out_ref, buf, wl, wt):
    factor = 1.0 / p_ref.shape[0]
    own = lax.axis_index("depth")
    prepare(p_ref, wl, wt, factor)
    fill(buf, guess_ref[...])
    run_forward(buf, guess_ref.shape[1], p_ref, wl, wt, factor * diff_ref[...], len_ref[own])
    out_ref[...] = inner(buf)


def tau_kernel(plan, len_ref, point_ref, p_ref, p2_ref, diff_ref, second_ref, *rest):
    msgs, (buf, wl, wt, whole) = rest[:-4], rest[-4:]
    most, _, rows = p_ref.shape
    factor = 1.0 / most
    own = lax.axis_index("depth")
    count = len_ref[jnp.minimum(own + 1, plan.count - 1)]
    width = point_ref.shape[1]
    prepare(p_ref, wl, wt, factor)
    fill(buf, point_ref[...])
    run_forward(buf, width, p_ref, wl, wt, factor * diff_ref[...], count)
    second_ref[...] = inner(buf)

    def coarse(q_ref, length):
        scale = length.astype(F32) * factor
        matrix = q_ref[0, :rows, :]
        forward_layer(
            buf, width, left_factor(matrix), left_factor((scale * matrix).T), bias_of(q_ref, 0),
            scale * diff_ref[...],
        )

    @pl.when(own > 0)
    def _():
        buf[:, LANES : LANES + width] = point_ref[...]
        coarse(p_ref, count)
        whole[...] = second_ref[...] - inner(buf)

    @pl.when(own == 0)
    def _():
        coarse(p2_ref, len_ref[2])
        whole[...] = inner(buf)

    size = plan.rows * IMG
    bias = bias_of(p_ref, 0)
    for shift, msg in enumerate(msgs):
        host = lax.rem(own - shift + 2 * plan.items, plan.items)
        start = plan.window(jnp.minimum(host, plan.hosts - 1))
        msg[:, 0:size] = whole[:, lanes(start, plan.rows)]
        msg[:, size : size + rows] = p_ref[0, :rows, :]
        msg[:, size + rows : size + rows + 1] = bias


def adjoint_kernel(
    len_ref, _, guess_ref, before_ref, after_ref, adj_ref, adj_after_ref,
    p_ref, p_before_ref, p_after_ref, diff_ref,
    point_ref, adj_out_ref, g_ref,
    buf, wl, wt, t_hi, t_lo, u_hi, u_lo,
):
    factor = 1.0 / p_ref.shape[0]
    own = lax.axis_index("depth")
    last = lax.axis_size("depth") - 1
    width = guess_ref.shape[1]
    spread = factor * diff_ref[...]
    g_ref[...] = jnp.zeros_like(g_ref)

    @pl.when(own < last)
    def _():
        count = len_ref[jnp.minimum(own + 1, last)]
        prepare(p_after_ref, wl, wt, factor)
        fill(buf, after_ref[...])
        run_forward(buf, width, p_after_ref, wl, wt, spread, count, (t_hi, t_lo))
        fill(buf, adj_after_ref[...])
        run_backward(buf, width, wl, wt, spread, count, (t_hi, t_lo))
        adj_out_ref[...] = inner(buf)

    @pl.when(own == last)
    def _():
        adj_out_ref[...] = adj_ref[...]

    @pl.when(own > 0)
    def _():
        count = len_ref[jnp.maximum(own - 1, 0)]
        prepare(p_before_ref, wl, wt, factor)
        fill(buf, before_ref[...])
        run_forward(buf, width, p_before_ref, wl, wt, spread, count)
        point_ref[...] = inner(buf)

    @pl.when(own == 0)
    def _():
        point_ref[...] = guess_ref[...]

    count = len_ref[own]
    prepare(p_ref, wl, wt, factor)
    fill(buf, point_ref[...])
    run_forward(buf, width, p_ref, wl, wt, spread, count, (t_hi, t_lo), (u_hi, u_lo))
    fill(buf, adj_out_ref[...])
    run_backward(
        buf, width, wl, wt, spread, count, (t_hi, t_lo), (u_hi, u_lo), (g_ref, factor)
    )
    adj_out_ref[...] = inner(buf)


def chain_kernel(plan, most, len_ref, _, second_ref, diff_ref, *rest):
    msgs, rest = rest[: plan.items], rest[plan.items :]
    outs, (buf, held, done, sem) = rest[: plan.results], rest[plan.results :]
    own = lax.axis_index("depth")
    host = own - plan.first
    rows = held.shape[1]
    size = plan.rows * IMG
    piece = plan.block * IMG

    @pl.when(jnp.logical_and(host >= 0, host < plan.hosts))
    def _():
        copies = [
            pltpu.make_async_copy(msg, held.at[lax.rem(host + shift, plan.items)], sem.at[shift])
            for shift, msg in enumerate(msgs)
        ]
        for copy in copies:
            copy.start()
        for copy in copies:
            copy.wait()
        offset = host * plan.block - plan.window(host)
        fill(buf, held[0, :, 0:size] + held[1, :, 0:size])

        def keep(result):
            done[result] = buf[:, pl.ds(pl.multiple_of(LANES + offset * IMG, LANES), piece)]

        keep(0)

        @pl.loop(2, plan.items)
        def _(item):
            scale = len_ref[item + 1].astype(F32) * (1.0 / most)
            matrix = held[item, :, size : size + rows]
            forward_layer(
                buf, size, left_factor(matrix), left_factor((scale * matrix).T),
                held[item, :, size + rows : size + rows + 1], scale * diff_ref[...],
            )
            buf[:, LANES : LANES + size] = inner(buf) + held[item, :, 0:size]
            keep(item - 1)

        for shift, out in enumerate(outs):
            out[...] = done[lax.rem(host + shift, plan.results)]

    @pl.when(own == 0)
    def _():
        for shift, out in enumerate(outs):
            if shift < plan.hosts:
                out[...] = second_ref[:, shift * piece : (shift + 1) * piece]


def collect_kernel(plan, point_ref, local_ref, *rest):
    received, out_ref = rest[:-1], rest[-1]
    own = lax.axis_index("depth")
    host = own - plan.first

    @pl.when(own < 2)
    def _():
        out_ref[...] = point_ref[...]

    @pl.when(own == 2)
    def _():
        for shift, block in enumerate(received):
            if shift < plan.hosts:
                out_ref[:, lanes(shift * plan.block, plan.block)] = block[...]

    for shift, block in enumerate(received):
        sender = lax.rem(own - 3 - shift + 2 * plan.results, plan.results)

        @pl.when(jnp.logical_and(own > 2, jnp.logical_and(sender < plan.hosts, sender != host)))
        def _():
            out_ref[:, lanes(sender * plan.block, plan.block)] = block[...]

    @pl.when(jnp.logical_and(own > 2, jnp.logical_and(host >= 0, host < plan.hosts)))
    def _():
        out_ref[:, lanes(host * plan.block, plan.block)] = local_ref[...]


SMEM = pl.BlockSpec(memory_space=pltpu.SMEM)
VMEM = pl.BlockSpec(memory_space=pltpu.VMEM)
ANY = pl.BlockSpec(memory_space=pl.ANY)


def call(kernel, out_shape, in_specs, scratch, micros, name):
    return pl.pallas_call(
        kernel,
        out_shape=out_shape,
        in_specs=in_specs,
        out_specs=jax.tree.map(lambda _: VMEM, out_shape),
        scratch_shapes=scratch,
        compiler_params=pltpu.CompilerParams(vmem_limit_bytes=48 * 2**20),
        cost_estimate=pl.CostEstimate(flops=int(micros * 1e9), bytes_accessed=2**21, transcendentals=0),
        name=name,
    )


def shifted(value, steps):
    count = lax.axis_size("depth")
    first, end = max(0, -steps), min(count, count - steps)
    return lax.ppermute(value, "depth", [(s, s + steps) for s in range(first, end)])


def batch_sum(value):
    count = lax.axis_size("batch")
    if count & (count - 1):
        return lax.psum(value, "batch")
    gap = 1
    while gap < count:
        value = value + lax.ppermute(value, "batch", [(s, s ^ gap) for s in range(count)])
        gap *= 2
    return value


def body(cpoint_guess, adjoint_guess, weights, biases, diffusion, section_len):
    plan = Plan(lax.axis_size("depth"))
    most, rows, _ = weights.shape
    width = cpoint_guess.shape[-1]
    guess, adjoint = cpoint_guess[0, 0], adjoint_guess[0, 0]
    diff = diffusion[:, None]

    def shape(*dims):
        return jax.ShapeDtypeStruct(dims, F32)

    state = shape(rows, width)
    buffer = pltpu.VMEM((rows, width + 2 * LANES), F32)
    factors = [pltpu.VMEM((most, rows, 3 * rows), BF16)] * 2

    packed = jnp.concatenate([weights, biases[:, None, :]], axis=1)
    packed_after = shifted(packed, -1)
    packed_second = lax.ppermute(packed[:1], "depth", [(2, 0)])
    before = shifted(guess, 1)
    adj_after = shifted(adjoint, -1)
    packed_before = shifted(packed, 1)

    after = call(push_kernel, state, [SMEM] + [VMEM] * 3, [buffer, *factors], 4, "push")(
        section_len, guess, packed, diff
    )
    window = shape(rows, plan.rows * IMG + LANES)
    second, *msgs = call(
        functools.partial(tau_kernel, plan), [state] + [window] * plan.items,
        [SMEM] + [VMEM] * 4, [buffer, *factors, pltpu.VMEM((rows, width), F32)], 3, "tau",
    )(section_len, after, packed_after, packed_second, diff)
    msgs = [
        msg if shift == plan.first else lax.ppermute(msg, "depth", plan.in_pairs(shift))
        for shift, msg in enumerate(msgs)
    ]

    saved = [pltpu.VMEM((most, rows, width), BF16)] * 4
    point, adjoint_out, grads = call(
        adjoint_kernel, [state, state, shape(most, rows, rows + 1)],
        [SMEM, ANY] + [VMEM] * 9, [buffer, *factors, *saved], 15, "adjoint",
    )(
        section_len, msgs[plan.first], guess, before, after, adjoint, adj_after,
        packed, packed_before, packed_after, diff,
    )

    blocks = call(
        functools.partial(chain_kernel, plan, most), [shape(rows, plan.block * IMG)] * plan.results,
        [SMEM, ANY, VMEM, VMEM] + [ANY] * plan.items,
        [
            pltpu.VMEM((rows, plan.rows * IMG + 2 * LANES), F32),
            pltpu.VMEM((plan.items, *window.shape), F32),
            pltpu.VMEM((plan.results, rows, plan.block * IMG), F32),
            pltpu.SemaphoreType.DMA((plan.items,)),
        ],
        1, "chain",
    )(section_len, grads, second, diff, *msgs)
    received = [lax.ppermute(block, "depth", plan.out_pairs(k)) for k, block in enumerate(blocks)]
    states = call(
        functools.partial(collect_kernel, plan), state, [VMEM] * (2 + plan.results), [], 0.5, "collect"
    )(point, blocks[plan.local], *received)

    grads = batch_sum(grads)
    return states[None, None], adjoint_out[None, None], grads[:, :, :rows], grads[:, :, rows]


def solution(mesh):
    state = P("depth", "batch", None, None)
    return jax.shard_map(
        body,
        mesh=mesh,
        in_specs=(state, state, P("depth", None, None), P("depth", None), P(), P()),
        out_specs=(state, state, P("depth", None, None), P("depth", None)),
        check_vma=False,
    )
```

time: 152 us -> 97.8 us (0.64)
  the two profiles are of different devices: /device:TPU:8 before, /device:TPU:26 now
where the time goes in v2:
time: 97.8 us; the launch traced here: 97.3 us
  waiting for transfers between devices  57 us (58%)
  starting transfers between devices  23.2 us (24%)
  Pallas kernels  12.6 us (13%)
  local copies, waits for them, and re-layouts  2.5 us (3%)
  other arithmetic  1.03 us (1%)
    ppermute x5, waiting for transfers between devices, body(): lax.ppermute(block, 'depth', plan.out_pairs(k))  43 us
    ppermute x4, waiting for transfers between devices, shifted(): lax.ppermute(value, 'depth', [(s, s + steps) for s in range(first, end)])  14 us
    ppermute x4, starting transfers between devices, shifted(): lax.ppermute(value, 'depth', [(s, s + steps) for s in range(first, end)])  11.7 us
    pallas_call x1, Pallas kernels, body(): call(adjoint_kernel, [state, state, shape(most, rows, rows + 1)], [SMEM,...  6.34 us
    ppermute x5, starting transfers between devices, body(): lax.ppermute(block, 'depth', plan.out_pairs(k))  5.84 us
    ppermute x5, starting transfers between devices, body(): lax.ppermute(msg, 'depth', plan.in_pairs(shift))  3.36 us
    pallas_call x1, Pallas kernels, body(): call(functools.partial(tau_kernel, plan), [state] + [window] * plan.items...  2.78 us
    pallas_call x1, Pallas kernels, body(): call(push_kernel, state, [SMEM] + [VMEM] * 3, [buffer, *factors], 4, 'push')  1.99 us
  transfers between devices with their start and end apart: 17, of which 6 were waited for; matrix products, arithmetic and copies ran while one was open for 1% of the time, Pallas kernels for 6%

profile of v2, /device:TPU:26, one launch (start us, length us, event | category | flops | bytes accessed | tf_op | source)
XLA Modules:
  0.0 97.3 jit_solution(15800241817439824113)
XLA Ops:
  0.7 1.0 %pad_maximum_fusion.p_ref = f32[8,33,32]{2,1,0:T(8,128)S(1)} fusion(f32[8,1,32]{2,1,0:T(1,128)} %bitcast.13, f32[8,32,32]{2,1,0:T(8,128)} %param.8), kind=kLoop, calls=%fused_computation.1 | loop fusion | flops 8448 | bytes 67584 | tf_op jit(solution)/shard_map/concatenate | solution.py:432
  1.6 1.3 %collective-permute-start.4 = (f32[8,33,32]{2,1,0:T(8,128)S(1)}, f32[8,33,32]{2,1,0:T(8,128)S(1)}, u32[]{:S(2)}, u32[]{:S(2)}) collective-permute-start(f32[8,33,32]{2,1,0:T(8,128)S(1)} %pad_maximum_fusion.p_ref), channel_id=1, source_target_pairs={{0,4},{4,8},{8,12},{12,16},{16,20},{20,24},{24,28},{1,5},{5,9},{9,... | collective-permute-start | bytes 101384 | tf_op jit(solution)/shard_map/ppermute | solution.py:404
  2.9 4.6 %collective-permute-start = (f32[8,33,32]{2,1,0:T(8,128)S(1)}, f32[8,33,32]{2,1,0:T(8,128)S(1)}, u32[]{:S(2)}, u32[]{:S(2)}) collective-permute-start(f32[8,33,32]{2,1,0:T(8,128)S(1)} %pad_maximum_fusion.p_ref), channel_id=1, source_target_pairs={{4,0},{8,4},{12,8},{16,12},{20,16},{24,20},{28,24},{5,1},{9,5},{13... | collective-permute-start | bytes 101384 | tf_op jit(solution)/shard_map/ppermute | solution.py:404
  8.2 1.3 %collective-permute-start.2 = (f32[32,4096]{1,0:T(8,128)}, f32[32,4096]{1,0:T(8,128)S(1)}, u32[]{:S(2)}, u32[]{:S(2)}) collective-permute-start(f32[32,4096]{1,0:T(8,128)} %bitcast.7), channel_id=1, source_target_pairs={{0,4},{4,8},{8,12},{12,16},{16,20},{20,24},{24,28},{1,5},{5,9},{9,... | collective-permute-start | bytes 1572872 | tf_op jit(solution)/shard_map/ppermute | solution.py:404
  9.5 4.6 %collective-permute-start.3 = (f32[32,4096]{1,0:T(8,128)}, f32[32,4096]{1,0:T(8,128)S(1)}, u32[]{:S(2)}, u32[]{:S(2)}) collective-permute-start(f32[32,4096]{1,0:T(8,128)} %bitcast.10), channel_id=1, source_target_pairs={{4,0},{8,4},{12,8},{16,12},{20,16},{24,20},{28,24},{5,1},{9,5},{13... | collective-permute-start | bytes 1572872 | tf_op jit(solution)/shard_map/ppermute | solution.py:404
  14.8 1.0 %copy-done = f32[1,1,32,4096]{3,2,1,0:T(8,128)S(1)} copy-done((f32[1,1,32,4096]{3,2,1,0:T(8,128)S(1)}, f32[1,1,32,4096]{3,2,1,0:T(8,128)}, u32[]{:S(2)}) %copy-start) | copy-done | bytes 524312
  15.8 2.0 %push.1.point_ref.after_ref = f32[32,4096]{1,0:T(8,128)S(1)} custom-call(s32[8]{0:T(128)S(1)} %copy-done.3, f32[32,4096]{1,0:T(8,128)S(1)} %bitcast.8, f32[8,33,32]{2,1,0:T(8,128)S(1)} %pad_maximum_fusion.p_ref, f32[32,1]{1,0:T(8,128)S(1)} %copy.14.diff_ref), custom_call_target="tpu_custom_call" | custom-call | flops 4000000000 | bytes 2097152 | tf_op jit(solution)/shard_map/push/pallas_call | solution.py:439
  17.9 2.8 %tau.1 = (f32[32,4096]{1,0:T(8,128)S(1)}, f32[32,1664]{1,0:T(8,128)S(1)}, f32[32,1664]{1,0:T(8,128)S(1)}, f32[32,1664]{1,0:T(8,128)S(1)}, f32[32,1664]{1,0:T(8,1...) custom-call(s32[8]{0:T(128)S(1)} %copy-done.3, f32[32,4096]{1,0:T(8,128)S(1)} %push.1.point_ref.after_ref, ...), custom_call_target="tpu_custom_call" | custom-call | flops 3000000000 | bytes 2097152 | tf_op jit(solution)/shard_map/tau/pallas_call | solution.py:443
  20.6 2.8 %collective-permute-done.2.before_ref = f32[32,4096]{1,0:T(8,128)S(1)} collective-permute-done((f32[32,4096]{1,0:T(8,128)}, f32[32,4096]{1,0:T(8,128)S(1)}, u32[]{:S(2)}, u32[]{:S(2)}) %collective-permute-start.2) | collective-permute-done | bytes 524320 | tf_op jit(solution)/shard_map/ppermute | solution.py:404
  23.4 11.2 %collective-permute-done.3.adj_after_ref = f32[32,4096]{1,0:T(8,128)S(1)} collective-permute-done((f32[32,4096]{1,0:T(8,128)}, f32[32,4096]{1,0:T(8,128)S(1)}, u32[]{:S(2)}, u32[]{:S(2)}) %collective-permute-start.3) | collective-permute-done | bytes 524320 | tf_op jit(solution)/shard_map/ppermute | solution.py:404
  34.6 6.3 %adjoint.1 = (f32[32,4096]{1,0:T(8,128)S(1)}, f32[32,4096]{1,0:T(8,128)}, f32[8,32,33]{2,1,0:T(8,128)S(1)}) custom-call(s32[8]{0:T(128)S(1)} %copy-done.3, f32[32,1664]{1,0:T(8,128)S(1)} %get-tuple-element.19._.rest_2_, f32[32,4096]{1,0:T(8,128)S(1)} %bitcast.9, f32[32,4096]{1,0:T(8,128)S(1)} %collective-permute-done.2.before_ref, ...), custom_call_target="tpu_custom_call" | custom-call | flops 15000000512 | bytes 2097152 | tf_op jit(solution)/shard_map/adjoint/pallas_call | solution.py:453
  41.6 0.7 collective-permute-start.6
  42.3 0.7 collective-permute-start.7
  44.4 1.6 %collective-permute-start.16 = (f32[8,32,33]{2,1,0:T(8,128)S(1)}, f32[8,32,33]{2,1,0:T(8,128)S(1)}, u32[]{:S(2)}, u32[]{:S(2)}) collective-permute-start(f32[8,32,33]{2,1,0:T(8,128)S(1)} %add.6), channel_id=1, source_target_pairs={{0,2},{1,3},{2,0},{3,1},{4,6},{5,7},{6,4},{7,5},{8,10},{9,11},{10,... | collective-permute-start | bytes 101384 | tf_op jit(solution)/shard_map/ppermute | solution.py:413
  47.3 1.3 %collective-permute-start.11 = (f32[32,1024]{1,0:T(8,128)S(1)}, f32[32,1024]{1,0:T(8,128)S(1)}, u32[]{:S(2)}, u32[]{:S(2)}) collective-permute-start(f32[32,1024]{1,0:T(8,128)S(1)} %get-tuple-element.30), channel_id=1, source_target_pairs={{8,16},{12,20},{16,24},{20,28},{0,8},{9,17},{13,21},{17,25},{21,29... | collective-permute-start | bytes 393224 | tf_op jit(solution)/shard_map/ppermute | solution.py:472
  48.6 1.3 %collective-permute-start.12 = (f32[32,1024]{1,0:T(8,128)S(1)}, f32[32,1024]{1,0:T(8,128)S(1)}, u32[]{:S(2)}, u32[]{:S(2)}) collective-permute-start(f32[32,1024]{1,0:T(8,128)S(1)} %get-tuple-element.31), channel_id=1, source_target_pairs={{8,20},{12,24},{16,28},{20,12},{0,8},{9,21},{13,25},{17,29},{21,13... | collective-permute-start | bytes 393224 | tf_op jit(solution)/shard_map/ppermute | solution.py:472
  49.9 1.3 %collective-permute-start.13 = (f32[32,1024]{1,0:T(8,128)S(1)}, f32[32,1024]{1,0:T(8,128)S(1)}, u32[]{:S(2)}, u32[]{:S(2)}) collective-permute-start(f32[32,1024]{1,0:T(8,128)S(1)} %get-tuple-element.32), channel_id=1, source_target_pairs={{8,24},{12,28},{16,12},{20,16},{0,8},{9,25},{13,29},{17,13},{21,17... | collective-permute-start | bytes 393224 | tf_op jit(solution)/shard_map/ppermute | solution.py:472
  51.2 1.3 %collective-permute-start.14 = (f32[32,1024]{1,0:T(8,128)S(1)}, f32[32,1024]{1,0:T(8,128)S(1)}, u32[]{:S(2)}, u32[]{:S(2)}) collective-permute-start(f32[32,1024]{1,0:T(8,128)S(1)} %get-tuple-element.28.local_ref), channel_id=1, source_target_pairs={{8,28},{9,29},{10,30},{11,31}} | collective-permute-start | bytes 393224 | tf_op jit(solution)/shard_map/ppermute | solution.py:472
  52.6 0.8 slice_reduce_fusion
  53.4 33.1 %collective-permute-done.11.rest_1_ = f32[32,1024]{1,0:T(8,128)S(1)} collective-permute-done((f32[32,1024]{1,0:T(8,128)S(1)}, f32[32,1024]{1,0:T(8,128)S(1)}, u32[]{:S(2)}, u32[]{:S(2)}) %collective-permute-start.11) | collective-permute-done | bytes 131104 | tf_op jit(solution)/shard_map/ppermute | solution.py:472
  86.5 3.1 %collective-permute-done.12.rest_2_ = f32[32,1024]{1,0:T(8,128)S(1)} collective-permute-done((f32[32,1024]{1,0:T(8,128)S(1)}, f32[32,1024]{1,0:T(8,128)S(1)}, u32[]{:S(2)}, u32[]{:S(2)}) %collective-permute-start.12) | collective-permute-done | bytes 131104 | tf_op jit(solution)/shard_map/ppermute | solution.py:472
  89.6 3.7 %collective-permute-done.13.rest_3_ = f32[32,1024]{1,0:T(8,128)S(1)} collective-permute-done((f32[32,1024]{1,0:T(8,128)S(1)}, f32[32,1024]{1,0:T(8,128)S(1)}, u32[]{:S(2)}, u32[]{:S(2)}) %collective-permute-start.13) | collective-permute-done | bytes 131104 | tf_op jit(solution)/shard_map/ppermute | solution.py:472
  93.3 3.1 %collective-permute-done.14.rest_4_ = f32[32,1024]{1,0:T(8,128)S(1)} collective-permute-done((f32[32,1024]{1,0:T(8,128)S(1)}, f32[32,1024]{1,0:T(8,128)S(1)}, u32[]{:S(2)}, u32[]{:S(2)}) %collective-permute-start.14) | collective-permute-done | bytes 131104 | tf_op jit(solution)/shard_map/ppermute | solution.py:472
  96.4 0.9 collect.1
  (37 shorter events, 4.8 us)
Async XLA Ops:
  0.6 6.9 %copy-start.4 = (f32[8,32,32]{2,1,0:T(8,128)S(1)}, f32[8,32,32]{2,1,0:T(8,128)}, u32[]{:S(2)}) copy-start(f32[8,32,32]{2,1,0:T(8,128)} %param.8) | copy-start | bytes 98308
  0.6 6.9 %copy-start.6 = (f32[8,32]{1,0:T(8,128)S(1)}, f32[8,32]{1,0:T(8,128)}, u32[]{:S(2)}) copy-start(f32[8,32]{1,0:T(8,128)} %param.9) | copy-start | bytes 3076
  1.6 19.0 %collective-permute-start.4 = (f32[8,33,32]{2,1,0:T(8,128)S(1)}, f32[8,33,32]{2,1,0:T(8,128)S(1)}, u32[]{:S(2)}, u32[]{:S(2)}) collective-permute-start(f32[8,33,32]{2,1,0:T(8,128)S(1)} %pad_maximum_fusion.p_ref), channel_id=1, source_target_pairs={{0,4},{4,8},{8,12},{12,16},{16,20},{20,24},{24,28},{1,5},{5,9},{9,... | collective-permute-start | bytes 101384 | tf_op jit(solution)/shard_map/ppermute | solution.py:404
  2.9 14.9 %collective-permute-start = (f32[8,33,32]{2,1,0:T(8,128)S(1)}, f32[8,33,32]{2,1,0:T(8,128)S(1)}, u32[]{:S(2)}, u32[]{:S(2)}) collective-permute-start(f32[8,33,32]{2,1,0:T(8,128)S(1)} %pad_maximum_fusion.p_ref), channel_id=1, source_target_pairs={{4,0},{8,4},{12,8},{16,12},{20,16},{24,20},{28,24},{5,1},{9,5},{13... | collective-permute-start | bytes 101384 | tf_op jit(solution)/shard_map/ppermute | solution.py:404
  7.5 10.3 %collective-permute-start.1 = (f32[1,33,32]{2,1,0:T(8,128)S(1)}, f32[1,33,32]{2,1,0:T(8,128)S(1)}, u32[]{:S(2)}, u32[]{:S(2)}) collective-permute-start(f32[1,33,32]{2,1,0:T(8,128)S(1)} %fusion), channel_id=1, source_target_pairs={{8,0},{9,1},{10,2},{11,3}} | collective-permute-start | bytes 12680 | tf_op jit(solution)/shard_map/ppermute | solution.py:434
  8.2 15.2 %collective-permute-start.2 = (f32[32,4096]{1,0:T(8,128)}, f32[32,4096]{1,0:T(8,128)S(1)}, u32[]{:S(2)}, u32[]{:S(2)}) collective-permute-start(f32[32,4096]{1,0:T(8,128)} %bitcast.7), channel_id=1, source_target_pairs={{0,4},{4,8},{8,12},{12,16},{16,20},{20,24},{24,28},{1,5},{5,9},{9,... | collective-permute-start | bytes 1572872 | tf_op jit(solution)/shard_map/ppermute | solution.py:404
  9.5 4.6 %copy-start.7 = (f32[32]{0:T(128)S(1)}, f32[32]{0:T(128)}, u32[]{:S(2)}) copy-start(f32[32]{0:T(128)} %param.10) | copy-start | bytes 388
  9.5 25.1 %collective-permute-start.3 = (f32[32,4096]{1,0:T(8,128)}, f32[32,4096]{1,0:T(8,128)S(1)}, u32[]{:S(2)}, u32[]{:S(2)}) collective-permute-start(f32[32,4096]{1,0:T(8,128)} %bitcast.10), channel_id=1, source_target_pairs={{4,0},{8,4},{12,8},{16,12},{20,16},{24,20},{28,24},{5,1},{9,5},{13... | collective-permute-start | bytes 1572872 | tf_op jit(solution)/shard_map/ppermute | solution.py:404
  14.8 1.0 %copy-start = (f32[1,1,32,4096]{3,2,1,0:T(8,128)S(1)}, f32[1,1,32,4096]{3,2,1,0:T(8,128)}, u32[]{:S(2)}) copy-start(f32[1,1,32,4096]{3,2,1,0:T(8,128)} %param.6) | copy-start | bytes 1572868
  17.8 16.8 %copy-start.1 = (f32[1,1,32,4096]{3,2,1,0:T(8,128)S(1)}, f32[1,1,32,4096]{3,2,1,0:T(8,128)}, u32[]{:S(2)}) copy-start(f32[1,1,32,4096]{3,2,1,0:T(8,128)} %param.6) | copy-start | bytes 1572868
  17.8 16.8 %copy-start.2 = (f32[1,1,32,4096]{3,2,1,0:T(8,128)S(1)}, f32[1,1,32,4096]{3,2,1,0:T(8,128)}, u32[]{:S(2)}) copy-start(f32[1,1,32,4096]{3,2,1,0:T(8,128)} %param.7) | copy-start | bytes 1572868
  40.9 2.7 %collective-permute-start.15 = (f32[8,32,33]{2,1,0:T(8,128)S(1)}, f32[8,32,33]{2,1,0:T(8,128)S(1)}, u32[]{:S(2)}, u32[]{:S(2)}) collective-permute-start(f32[8,32,33]{2,1,0:T(8,128)S(1)} %get-tuple-element.21._), channel_id=1, source_target_pairs={{0,1},{1,0},{2,3},{3,2},{4,5},{5,4},{6,7},{7,6},{8,9},{9,8},{10,11... | collective-permute-start | bytes 101384 | tf_op jit(solution)/shard_map/ppermute | solution.py:413
  41.0 3.4 %collective-permute-start.5 = (f32[32,1664]{1,0:T(8,128)S(1)}, f32[32,1664]{1,0:T(8,128)S(1)}, u32[]{:S(2)}, u32[]{:S(2)}) collective-permute-start(f32[32,1664]{1,0:T(8,128)S(1)} %get-tuple-element.23), channel_id=1, source_target_pairs={{0,8},{4,12},{8,16},{12,20},{1,9},{5,13},{9,17},{13,21},{2,10},{6,... | collective-permute-start | bytes 638984 | tf_op jit(solution)/shard_map/ppermute | solution.py:448
  41.6 4.4 %collective-permute-start.6 = (f32[32,1664]{1,0:T(8,128)S(1)}, f32[32,1664]{1,0:T(8,128)S(1)}, u32[]{:S(2)}, u32[]{:S(2)}) collective-permute-start(f32[32,1664]{1,0:T(8,128)S(1)} %get-tuple-element.24), channel_id=1, source_target_pairs={{4,8},{8,12},{12,16},{16,20},{5,9},{9,13},{13,17},{17,21},{6,10},{... | collective-permute-start | bytes 638984 | tf_op jit(solution)/shard_map/ppermute | solution.py:448
  42.3 3.7 %collective-permute-start.7 = (f32[32,1664]{1,0:T(8,128)S(1)}, f32[32,1664]{1,0:T(8,128)S(1)}, u32[]{:S(2)}, u32[]{:S(2)}) collective-permute-start(f32[32,1664]{1,0:T(8,128)S(1)} %get-tuple-element.25), channel_id=1, source_target_pairs={{12,8},{16,12},{20,16},{0,20},{13,9},{17,13},{21,17},{1,21},{14,10... | collective-permute-start | bytes 638984 | tf_op jit(solution)/shard_map/ppermute | solution.py:448
  43.0 3.0 %collective-permute-start.8 = (f32[32,1664]{1,0:T(8,128)S(1)}, f32[32,1664]{1,0:T(8,128)S(1)}, u32[]{:S(2)}, u32[]{:S(2)}) collective-permute-start(f32[32,1664]{1,0:T(8,128)S(1)} %get-tuple-element.26), channel_id=1, source_target_pairs={{16,8},{20,12},{0,16},{4,20},{17,9},{21,13},{1,17},{5,21},{18,10},... | collective-permute-start | bytes 638984 | tf_op jit(solution)/shard_map/ppermute | solution.py:448
  43.7 2.3 %collective-permute-start.9 = (f32[32,1664]{1,0:T(8,128)S(1)}, f32[32,1664]{1,0:T(8,128)S(1)}, u32[]{:S(2)}, u32[]{:S(2)}) collective-permute-start(f32[32,1664]{1,0:T(8,128)S(1)} %get-tuple-element.27), channel_id=1, source_target_pairs={{20,8},{0,12},{4,16},{8,20},{21,9},{1,13},{5,17},{9,21},{22,10},{2... | collective-permute-start | bytes 638984 | tf_op jit(solution)/shard_map/ppermute | solution.py:448
  44.4 6.8 %collective-permute-start.16 = (f32[8,32,33]{2,1,0:T(8,128)S(1)}, f32[8,32,33]{2,1,0:T(8,128)S(1)}, u32[]{:S(2)}, u32[]{:S(2)}) collective-permute-start(f32[8,32,33]{2,1,0:T(8,128)S(1)} %add.6), channel_id=1, source_target_pairs={{0,2},{1,3},{2,0},{3,1},{4,6},{5,7},{6,4},{7,5},{8,10},{9,11},{10,... | collective-permute-start | bytes 101384 | tf_op jit(solution)/shard_map/ppermute | solution.py:413
  46.7 6.7 %collective-permute-start.10 = (f32[32,1024]{1,0:T(8,128)S(1)}, f32[32,1024]{1,0:T(8,128)S(1)}, u32[]{:S(2)}, u32[]{:S(2)}) collective-permute-start(f32[32,1024]{1,0:T(8,128)S(1)} %get-tuple-element.29), channel_id=1, source_target_pairs={{8,12},{12,16},{16,20},{20,24},{0,8},{9,13},{13,17},{17,21},{21,25... | collective-permute-start | bytes 393224 | tf_op jit(solution)/shard_map/ppermute | solution.py:472
  47.3 39.2 %collective-permute-start.11 = (f32[32,1024]{1,0:T(8,128)S(1)}, f32[32,1024]{1,0:T(8,128)S(1)}, u32[]{:S(2)}, u32[]{:S(2)}) collective-permute-start(f32[32,1024]{1,0:T(8,128)S(1)} %get-tuple-element.30), channel_id=1, source_target_pairs={{8,16},{12,20},{16,24},{20,28},{0,8},{9,17},{13,21},{17,25},{21,29... | collective-permute-start | bytes 393224 | tf_op jit(solution)/shard_map/ppermute | solution.py:472
  48.6 41.0 %collective-permute-start.12 = (f32[32,1024]{1,0:T(8,128)S(1)}, f32[32,1024]{1,0:T(8,128)S(1)}, u32[]{:S(2)}, u32[]{:S(2)}) collective-permute-start(f32[32,1024]{1,0:T(8,128)S(1)} %get-tuple-element.31), channel_id=1, source_target_pairs={{8,20},{12,24},{16,28},{20,12},{0,8},{9,21},{13,25},{17,29},{21,13... | collective-permute-start | bytes 393224 | tf_op jit(solution)/shard_map/ppermute | solution.py:472
  49.9 43.3 %collective-permute-start.13 = (f32[32,1024]{1,0:T(8,128)S(1)}, f32[32,1024]{1,0:T(8,128)S(1)}, u32[]{:S(2)}, u32[]{:S(2)}) collective-permute-start(f32[32,1024]{1,0:T(8,128)S(1)} %get-tuple-element.32), channel_id=1, source_target_pairs={{8,24},{12,28},{16,12},{20,16},{0,8},{9,25},{13,29},{17,13},{21,17... | collective-permute-start | bytes 393224 | tf_op jit(solution)/shard_map/ppermute | solution.py:472
  51.2 45.1 %collective-permute-start.14 = (f32[32,1024]{1,0:T(8,128)S(1)}, f32[32,1024]{1,0:T(8,128)S(1)}, u32[]{:S(2)}, u32[]{:S(2)}) collective-permute-start(f32[32,1024]{1,0:T(8,128)S(1)} %get-tuple-element.28.local_ref), channel_id=1, source_target_pairs={{8,28},{9,29},{10,30},{11,31}} | collective-permute-start | bytes 393224 | tf_op jit(solution)/shard_map/ppermute | solution.py:472
  52.6 44.7 %copy-start.5 = (f32[8,32,33]{2,1,0:T(8,128)}, f32[8,32,33]{2,1,0:T(8,128)S(1)}, u32[]{:S(2)}) copy-start(f32[8,32,33]{2,1,0:T(8,128)S(1)} %add.7) | copy-start | bytes 101380
  (1 other events, 0.7 us)

commit v3 on v2

--- a/solution.py
+++ b/solution.py
@@ -11,6 +11,7 @@
 LANES = 128
 CHUNK = 256
 GRAD_CHUNK = 2048
+AT_ONCE = 4
 F32 = jnp.float32
 BF16 = jnp.bfloat16
 
@@ -255,32 +256,14 @@
         msg[:, size + rows : size + rows + 1] = bias
 
 
-def adjoint_kernel(
-    len_ref, _, guess_ref, before_ref, after_ref, adj_ref, adj_after_ref,
-    p_ref, p_before_ref, p_after_ref, diff_ref,
-    point_ref, adj_out_ref, g_ref,
-    buf, wl, wt, t_hi, t_lo, u_hi, u_lo,
+def point_kernel(
+    len_ref, _, guess_ref, before_ref, p_ref, p_before_ref, diff_ref,
+    point_ref, t_hi, t_lo, u_hi, u_lo, buf, wl, wt,
 ):
     factor = 1.0 / p_ref.shape[0]
     own = lax.axis_index("depth")
-    last = lax.axis_size("depth") - 1
     width = guess_ref.shape[1]
     spread = factor * diff_ref[...]
-    g_ref[...] = jnp.zeros_like(g_ref)
-
-    @pl.when(own < last)
-    def _():
-        count = len_ref[jnp.minimum(own + 1, last)]
-        prepare(p_after_ref, wl, wt, factor)
-        fill(buf, after_ref[...])
-        run_forward(buf, width, p_after_ref, wl, wt, spread, count, (t_hi, t_lo))
-        fill(buf, adj_after_ref[...])
-        run_backward(buf, width, wl, wt, spread, count, (t_hi, t_lo))
-        adj_out_ref[...] = inner(buf)
-
-    @pl.when(own == last)
-    def _():
-        adj_out_ref[...] = adj_ref[...]
 
     @pl.when(own > 0)
     def _():
@@ -293,14 +276,39 @@
     @pl.when(own == 0)
     def _():
         point_ref[...] = guess_ref[...]
-
-    count = len_ref[own]
+        fill(buf, guess_ref[...])
+
     prepare(p_ref, wl, wt, factor)
-    fill(buf, point_ref[...])
-    run_forward(buf, width, p_ref, wl, wt, spread, count, (t_hi, t_lo), (u_hi, u_lo))
-    fill(buf, adj_out_ref[...])
+    run_forward(buf, width, p_ref, wl, wt, spread, len_ref[own], (t_hi, t_lo), (u_hi, u_lo))
+
+
+def adjoint_kernel(
+    len_ref, after_ref, adj_ref, adj_after_ref, p_ref, p_after_ref, diff_ref, t_hi, t_lo, u_hi, u_lo,
+    adj_out_ref, g_ref, buf, wl, wt, t_next_hi, t_next_lo,
+):
+    factor = 1.0 / p_ref.shape[0]
+    own = lax.axis_index("depth")
+    last = lax.axis_size("depth") - 1
+    width = after_ref.shape[1]
+    spread = factor * diff_ref[...]
+    g_ref[...] = jnp.zeros_like(g_ref)
+
+    @pl.when(own < last)
+    def _():
+        count = len_ref[jnp.minimum(own + 1, last)]
+        prepare(p_after_ref, wl, wt, factor)
+        fill(buf, after_ref[...])
+        run_forward(buf, width, p_after_ref, wl, wt, spread, count, (t_next_hi, t_next_lo))
+        fill(buf, adj_after_ref[...])
+        run_backward(buf, width, wl, wt, spread, count, (t_next_hi, t_next_lo))
+
+    @pl.when(own == last)
+    def _():
+        fill(buf, adj_ref[...])
+
+    prepare(p_ref, wl, wt, factor)
     run_backward(
-        buf, width, wl, wt, spread, count, (t_hi, t_lo), (u_hi, u_lo), (g_ref, factor)
+        buf, width, wl, wt, spread, len_ref[own], (t_hi, t_lo), (u_hi, u_lo), (g_ref, factor)
     )
     adj_out_ref[...] = inner(buf)
 
@@ -392,8 +400,8 @@
         in_specs=in_specs,
         out_specs=jax.tree.map(lambda _: VMEM, out_shape),
         scratch_shapes=scratch,
-        compiler_params=pltpu.CompilerParams(vmem_limit_bytes=48 * 2**20),
-        cost_estimate=pl.CostEstimate(flops=int(micros * 1e9), bytes_accessed=2**21, transcendentals=0),
+        compiler_params=pltpu.CompilerParams(vmem_limit_bytes=32 * 2**20),
+        cost_estimate=pl.CostEstimate(flops=int(micros * 1e8), bytes_accessed=2**21, transcendentals=0),
         name=name,
     )
 
@@ -431,32 +439,41 @@
 
     packed = jnp.concatenate([weights, biases[:, None, :]], axis=1)
     packed_after = shifted(packed, -1)
-    packed_second = lax.ppermute(packed[:1], "depth", [(2, 0)])
     before = shifted(guess, 1)
-    adj_after = shifted(adjoint, -1)
-    packed_before = shifted(packed, 1)
-
-    after = call(push_kernel, state, [SMEM] + [VMEM] * 3, [buffer, *factors], 4, "push")(
+
+    after = call(push_kernel, state, [SMEM] + [VMEM] * 3, [buffer, *factors], 40, "push")(
         section_len, guess, packed, diff
     )
+    after, packed_after, packed_later, adjoint_later = lax.optimization_barrier(
+        (after, packed_after, packed, adjoint)
+    )
+    packed_second = lax.ppermute(packed_later[:1], "depth", [(2, 0)])
+    packed_before = shifted(packed_later, 1)
+    adj_after = shifted(adjoint_later, -1)
+
     window = shape(rows, plan.rows * IMG + LANES)
     second, *msgs = call(
         functools.partial(tau_kernel, plan), [state] + [window] * plan.items,
         [SMEM] + [VMEM] * 4, [buffer, *factors, pltpu.VMEM((rows, width), F32)], 3, "tau",
     )(section_len, after, packed_after, packed_second, diff)
-    msgs = [
-        msg if shift == plan.first else lax.ppermute(msg, "depth", plan.in_pairs(shift))
-        for shift, msg in enumerate(msgs)
-    ]
-
-    saved = [pltpu.VMEM((most, rows, width), BF16)] * 4
-    point, adjoint_out, grads = call(
-        adjoint_kernel, [state, state, shape(most, rows, rows + 1)],
-        [SMEM, ANY] + [VMEM] * 9, [buffer, *factors, *saved], 15, "adjoint",
-    )(
-        section_len, msgs[plan.first], guess, before, after, adjoint, adj_after,
-        packed, packed_before, packed_after, diff,
-    )
+    msgs, before, packed_before = lax.optimization_barrier((msgs, before, packed_before))
+    arrived = {plan.first: msgs[plan.first]}
+    order = [shift for shift in range(plan.items) if shift != plan.first]
+    for k, shift in enumerate(order):
+        msg = msgs[shift]
+        if k >= AT_ONCE:
+            msg, _ = lax.optimization_barrier((msg, arrived[order[k - AT_ONCE]]))
+        arrived[shift] = lax.ppermute(msg, "depth", plan.in_pairs(shift))
+    msgs = [arrived[shift] for shift in range(plan.items)]
+
+    saved = jax.ShapeDtypeStruct((most, rows, width), BF16)
+    point, *states = call(
+        point_kernel, [state] + [saved] * 4, [SMEM, ANY] + [VMEM] * 5, [buffer, *factors], 6, "point"
+    )(section_len, msgs[plan.first], guess, before, packed, packed_before, diff)
+    adjoint_out, grads = call(
+        adjoint_kernel, [state, shape(most, rows, rows + 1)],
+        [SMEM] + [VMEM] * 10, [buffer, *factors] + [pltpu.VMEM(saved.shape, BF16)] * 2, 10, "adjoint",
+    )(section_len, after, adjoint, adj_after, packed, packed_after, diff, *states)
 
     blocks = call(
         functools.partial(chain_kernel, plan, most), [shape(rows, plan.block * IMG)] * plan.results,
@@ -474,6 +491,7 @@
         functools.partial(collect_kernel, plan), state, [VMEM] * (2 + plan.results), [], 0.5, "collect"
     )(point, blocks[plan.local], *received)
 
+    _, grads = lax.optimization_barrier((received[0], grads))
     grads = batch_sum(grads)
     return states[None, None], adjoint_out[None, None], grads[:, :, :rows], grads[:, :, rows]
 

time: 97.8 us -> 95.5 us (0.976)
  the two profiles are of different devices: /device:TPU:26 before, /device:TPU:0 now
where the time goes in v3:
time: 95.5 us; the launch traced here: 94.9 us
  starting transfers between devices  57.6 us (60%)
  waiting for transfers between devices  17.6 us (18%)
  Pallas kernels  14.6 us (15%)
  local copies, waits for them, and re-layouts  3.23 us (3%)
  other arithmetic  0.97 us (1%)
    ppermute x5, starting transfers between devices, body(): lax.ppermute(block, 'depth', plan.out_pairs(k))  25.1 us
    ppermute x5, starting transfers between devices, body(): arrived[shift] = lax.ppermute(msg, 'depth', plan.in_pairs(shift))  16 us
    ppermute x4, starting transfers between devices, shifted(): lax.ppermute(value, 'depth', [(s, s + steps) for s in range(first, end)])  13.5 us
    ppermute x1, waiting for transfers between devices, body(): packed_second = lax.ppermute(packed_later[:1], 'depth', [(2, 0)])  9.75 us
    pallas_call x1, Pallas kernels, body(): call(adjoint_kernel, [state, shape(most, rows, rows + 1)], [SMEM] + [VMEM...  6.26 us
    ppermute x2, waiting for transfers between devices, batch_sum(): lax.ppermute(value, 'batch', [(s, s ^ gap) for s in range(count)])  4.42 us
    ppermute x4, waiting for transfers between devices, shifted(): lax.ppermute(value, 'depth', [(s, s + steps) for s in range(first, end)])  3.36 us
    pallas_call x1, Pallas kernels, body(): call(functools.partial(tau_kernel, plan), [state] + [window] * plan.items...  2.74 us
  transfers between devices with their start and end apart: 17, of which 4 were waited for; matrix products, arithmetic and copies ran while one was open for 1% of the time, Pallas kernels for 15%

profile of v3, /device:TPU:0, one launch (start us, length us, event | category | flops | bytes accessed | tf_op | source)
XLA Modules:
  0.0 94.9 jit_solution(4246236165992690864)
XLA Ops:
  0.6 0.9 pad_maximum_fusion.p_ref
  1.6 1.3 %collective-permute-start = (f32[8,33,32]{2,1,0:T(8,128)S(1)}, f32[8,33,32]{2,1,0:T(8,128)S(1)}, u32[]{:S(2)}, u32[]{:S(2)}) collective-permute-start(f32[8,33,32]{2,1,0:T(8,128)S(1)} %pad_maximum_fusion.p_ref), channel_id=1, source_target_pairs={{4,0},{8,4},{12,8},{16,12},{20,16},{24,20},{28,24},{5,1},{9,5},{13... | collective-permute-start | bytes 101384 | tf_op jit(solution)/shard_map/ppermute | solution.py:412
  2.9 5.5 %collective-permute-start.2 = (f32[32,4096]{1,0:T(8,128)}, f32[32,4096]{1,0:T(8,128)S(1)}, u32[]{:S(2)}, u32[]{:S(2)}) collective-permute-start(f32[32,4096]{1,0:T(8,128)} %bitcast.9), channel_id=1, source_target_pairs={{0,4},{4,8},{8,12},{12,16},{16,20},{20,24},{24,28},{1,5},{5,9},{9,... | collective-permute-start | bytes 1572872 | tf_op jit(solution)/shard_map/ppermute | solution.py:412
  9.8 1.0 %copy-done.2 = f32[1,1,32,4096]{3,2,1,0:T(8,128)S(1)} copy-done((f32[1,1,32,4096]{3,2,1,0:T(8,128)S(1)}, f32[1,1,32,4096]{3,2,1,0:T(8,128)}, u32[]{:S(2)}) %copy-start.2) | copy-done | bytes 524312
  10.8 2.0 %push.1.point_ref.after_ref = f32[32,4096]{1,0:T(8,128)S(1)} custom-call(s32[8]{0:T(128)S(1)} %copy-done.1, f32[32,4096]{1,0:T(8,128)S(1)} %bitcast.10, f32[8,33,32]{2,1,0:T(8,128)S(1)} %pad_maximum_fusion.p_ref, f32[32,1]{1,0:T(8,128)S(1)} %copy.15.diff_ref), custom_call_target="tpu_custom_call" | custom-call | flops 4000000000 | bytes 2097152 | tf_op jit(solution)/shard_map/push/pallas_call | solution.py:444
  12.8 1.3 %collective-permute-start.4 = (f32[32,4096]{1,0:T(8,128)S(1)}, f32[32,4096]{1,0:T(8,128)S(1)}, u32[]{:S(2)}, u32[]{:S(2)}) collective-permute-start(f32[32,4096]{1,0:T(8,128)S(1)} %bitcast.7), channel_id=1, source_target_pairs={{4,0},{8,4},{12,8},{16,12},{20,16},{24,20},{28,24},{5,1},{9,5},{13... | collective-permute-start | bytes 1572872 | tf_op jit(solution)/shard_map/ppermute | solution.py:412
  14.1 5.4 %collective-permute-start.3 = (f32[8,33,32]{2,1,0:T(8,128)S(1)}, f32[8,33,32]{2,1,0:T(8,128)S(1)}, u32[]{:S(2)}, u32[]{:S(2)}) collective-permute-start(f32[8,33,32]{2,1,0:T(8,128)S(1)} %pad_maximum_fusion.p_ref), channel_id=1, source_target_pairs={{0,4},{4,8},{8,12},{12,16},{16,20},{20,24},{24,28},{1,5},{5,9},{9,... | collective-permute-start | bytes 101384 | tf_op jit(solution)/shard_map/ppermute | solution.py:412
  19.6 1.3 %collective-permute-start.1 = (f32[1,33,32]{2,1,0:T(8,128)S(1)}, f32[1,33,32]{2,1,0:T(8,128)S(1)}, u32[]{:S(2)}, u32[]{:S(2)}) collective-permute-start(f32[1,33,32]{2,1,0:T(8,128)S(1)} %slice.9), channel_id=1, source_target_pairs={{8,0},{9,1},{10,2},{11,3}} | collective-permute-start | bytes 12680 | tf_op jit(solution)/shard_map/ppermute | solution.py:450
  20.9 9.8 %collective-permute-done.1.p2_ref = f32[1,33,32]{2,1,0:T(8,128)S(1)} collective-permute-done((f32[1,33,32]{2,1,0:T(8,128)S(1)}, f32[1,33,32]{2,1,0:T(8,128)S(1)}, u32[]{:S(2)}, u32[]{:S(2)}) %collective-permute-start.1) | collective-permute-done | bytes 4256 | tf_op jit(solution)/shard_map/ppermute | solution.py:450
  30.6 2.7 %tau.1 = (f32[32,4096]{1,0:T(8,128)S(1)}, f32[32,1664]{1,0:T(8,128)S(1)}, f32[32,1664]{1,0:T(8,128)S(1)}, f32[32,1664]{1,0:T(8,128)S(1)}, f32[32,1664]{1,0:T(8,1...) custom-call(s32[8]{0:T(128)S(1)} %copy-done.1, f32[32,4096]{1,0:T(8,128)S(1)} %push.1.point_ref.after_ref, ...), custom_call_target="tpu_custom_call" | custom-call | flops 300000000 | bytes 2097152 | tf_op jit(solution)/shard_map/tau/pallas_call | solution.py:455
  33.4 3.3 %collective-permute-done.3.p_before_ref = f32[8,33,32]{2,1,0:T(8,128)S(1)} collective-permute-done((f32[8,33,32]{2,1,0:T(8,128)S(1)}, f32[8,33,32]{2,1,0:T(8,128)S(1)}, u32[]{:S(2)}, u32[]{:S(2)}) %collective-permute-start.3) | collective-permute-done | bytes 33824 | tf_op jit(solution)/shard_map/ppermute | solution.py:412
  36.7 3.5 %collective-permute-start.5 = (f32[32,1664]{1,0:T(8,128)S(1)}, f32[32,1664]{1,0:T(8,128)S(1)}, u32[]{:S(2)}, u32[]{:S(2)}) collective-permute-start(f32[32,1664]{1,0:T(8,128)S(1)} %get-tuple-element.57), channel_id=1, source_target_pairs={{0,8},{4,12},{8,16},{12,20},{1,9},{5,13},{9,17},{13,21},{2,10},{6,... | collective-permute-start | bytes 638984 | tf_op jit(solution)/shard_map/ppermute | solution.py:466
  40.9 4.8 %collective-permute-start.7 = (f32[32,1664]{1,0:T(8,128)S(1)}, f32[32,1664]{1,0:T(8,128)S(1)}, u32[]{:S(2)}, u32[]{:S(2)}) collective-permute-start(f32[32,1664]{1,0:T(8,128)S(1)} %get-tuple-element.59), channel_id=1, source_target_pairs={{12,8},{16,12},{20,16},{0,20},{13,9},{17,13},{21,17},{1,21},{14,10... | collective-permute-start | bytes 638984 | tf_op jit(solution)/shard_map/ppermute | solution.py:466
  45.8 5.2 %collective-permute-start.8 = (f32[32,1664]{1,0:T(8,128)S(1)}, f32[32,1664]{1,0:T(8,128)S(1)}, u32[]{:S(2)}, u32[]{:S(2)}) collective-permute-start(f32[32,1664]{1,0:T(8,128)S(1)} %get-tuple-element.60), channel_id=1, source_target_pairs={{16,8},{20,12},{0,16},{4,20},{17,9},{21,13},{1,17},{5,21},{18,10},... | collective-permute-start | bytes 638984 | tf_op jit(solution)/shard_map/ppermute | solution.py:466
  51.0 1.8 %collective-permute-start.9 = (f32[32,1664]{1,0:T(8,128)S(1)}, f32[32,1664]{1,0:T(8,128)S(1)}, u32[]{:S(2)}, u32[]{:S(2)}) collective-permute-start(f32[32,1664]{1,0:T(8,128)S(1)} %get-tuple-element.62), channel_id=1, source_target_pairs={{20,8},{0,12},{4,16},{8,20},{21,9},{1,13},{5,17},{9,21},{22,10},{2... | collective-permute-start | bytes 638984 | tf_op jit(solution)/shard_map/ppermute | solution.py:466
  52.8 2.1 %point.1 = (f32[32,4096]{1,0:T(8,128)S(1)}, bf16[8,32,4096]{2,1,0:T(8,128)(2,1)S(1)}, bf16[8,32,4096]{2,1,0:T(8,128)(2,1)S(1)}, bf16[8,32,4096]{2,1,0:T(8,128)(2,1)S(1)}, bf16[8,32,4096]{2,1,0:T(8,128)(2,1)S(1)}) custom-call(s32[8]{0:T(128)S(1)} %copy-done.1, f32[32,1664]{1,0:T(8,128)S(1)} %get-tuple-element.46._.rest_2_, f32[32,4096]{1,0:T(8,128)S(1)} %bitcast.11, ...), custom_call_target="tpu_custom_call" | custom-call | flops 600000000 | bytes 2097152 | tf_op jit(solution)/shard_map/point/pallas_call | solution.py:470
  54.9 6.3 %adjoint.1 = (f32[32,4096]{1,0:T(8,128)}, f32[8,32,33]{2,1,0:T(8,128)S(1)}) custom-call(s32[8]{0:T(128)S(1)} %copy-done.1, f32[32,4096]{1,0:T(8,128)S(1)} %push.1.point_ref.after_ref, f32[32,4096]{1,0:T(8,128)S(1)} %bitcast.8, f32[32,4096]{1,0:T(8,128)S(1)} %collective-permute-done.4.adj_after_ref, f32[8,33,32]{2,1,0:T(8,128)S(1)} %pad_maximum_fusion.p_ref, ...), custom_call_target="tpu_custom_call" | custom-call | flops 1000000000 | bytes 2097152 | tf_op jit(solution)/shard_map/adjoint/pallas_call | solution.py:473
  61.9 10.9 %collective-permute-start.10 = (f32[32,1024]{1,0:T(8,128)S(1)}, f32[32,1024]{1,0:T(8,128)S(1)}, u32[]{:S(2)}, u32[]{:S(2)}) collective-permute-start(f32[32,1024]{1,0:T(8,128)S(1)} %get-tuple-element.64), channel_id=1, source_target_pairs={{8,12},{12,16},{16,20},{20,24},{0,8},{9,13},{13,17},{17,21},{21,25... | collective-permute-start | bytes 393224 | tf_op jit(solution)/shard_map/ppermute | solution.py:489
  72.8 1.9 %collective-permute-start.11 = (f32[32,1024]{1,0:T(8,128)S(1)}, f32[32,1024]{1,0:T(8,128)S(1)}, u32[]{:S(2)}, u32[]{:S(2)}) collective-permute-start(f32[32,1024]{1,0:T(8,128)S(1)} %get-tuple-element.65), channel_id=1, source_target_pairs={{8,16},{12,20},{16,24},{20,28},{0,8},{9,17},{13,21},{17,25},{21,29... | collective-permute-start | bytes 393224 | tf_op jit(solution)/shard_map/ppermute | solution.py:489
  74.7 9.7 %collective-permute-start.12 = (f32[32,1024]{1,0:T(8,128)S(1)}, f32[32,1024]{1,0:T(8,128)S(1)}, u32[]{:S(2)}, u32[]{:S(2)}) collective-permute-start(f32[32,1024]{1,0:T(8,128)S(1)} %get-tuple-element.66), channel_id=1, source_target_pairs={{8,20},{12,24},{16,28},{20,12},{0,8},{9,21},{13,25},{17,29},{21,13... | collective-permute-start | bytes 393224 | tf_op jit(solution)/shard_map/ppermute | solution.py:489
  84.4 1.9 %collective-permute-start.13 = (f32[32,1024]{1,0:T(8,128)S(1)}, f32[32,1024]{1,0:T(8,128)S(1)}, u32[]{:S(2)}, u32[]{:S(2)}) collective-permute-start(f32[32,1024]{1,0:T(8,128)S(1)} %get-tuple-element.67), channel_id=1, source_target_pairs={{8,24},{12,28},{16,12},{20,16},{0,8},{9,25},{13,29},{17,13},{21,17... | collective-permute-start | bytes 393224 | tf_op jit(solution)/shard_map/ppermute | solution.py:489
  87.1 1.3 %collective-permute-done.15 = f32[8,32,33]{2,1,0:T(8,128)S(1)} collective-permute-done((f32[8,32,33]{2,1,0:T(8,128)S(1)}, f32[8,32,33]{2,1,0:T(8,128)S(1)}, u32[]{:S(2)}, u32[]{:S(2)}) %collective-permute-start.15) | collective-permute-done | bytes 33824 | tf_op jit(solution)/shard_map/ppermute | solution.py:421
  88.4 1.6 %collective-permute-start.16 = (f32[8,32,33]{2,1,0:T(8,128)S(1)}, f32[8,32,33]{2,1,0:T(8,128)S(1)}, u32[]{:S(2)}, u32[]{:S(2)}) collective-permute-start(f32[8,32,33]{2,1,0:T(8,128)S(1)} %add.6), channel_id=1, source_target_pairs={{0,2},{1,3},{2,0},{3,1},{4,6},{5,7},{6,4},{7,5},{8,10},{9,11},{10,... | collective-permute-start | bytes 101384 | tf_op jit(solution)/shard_map/ppermute | solution.py:421
  91.0 3.1 %collective-permute-done.16 = f32[8,32,33]{2,1,0:T(8,128)S(1)} collective-permute-done((f32[8,32,33]{2,1,0:T(8,128)S(1)}, f32[8,32,33]{2,1,0:T(8,128)S(1)}, u32[]{:S(2)}, u32[]{:S(2)}) %collective-permute-start.16) | collective-permute-done | bytes 33824 | tf_op jit(solution)/shard_map/ppermute | solution.py:421
  (32 shorter events, 5.3 us)
Async XLA Ops:
  1.6 11.3 %collective-permute-start = (f32[8,33,32]{2,1,0:T(8,128)S(1)}, f32[8,33,32]{2,1,0:T(8,128)S(1)}, u32[]{:S(2)}, u32[]{:S(2)}) collective-permute-start(f32[8,33,32]{2,1,0:T(8,128)S(1)} %pad_maximum_fusion.p_ref), channel_id=1, source_target_pairs={{4,0},{8,4},{12,8},{16,12},{20,16},{24,20},{28,24},{5,1},{9,5},{13... | collective-permute-start | bytes 101384 | tf_op jit(solution)/shard_map/ppermute | solution.py:412
  2.9 33.9 %collective-permute-start.2 = (f32[32,4096]{1,0:T(8,128)}, f32[32,4096]{1,0:T(8,128)S(1)}, u32[]{:S(2)}, u32[]{:S(2)}) collective-permute-start(f32[32,4096]{1,0:T(8,128)} %bitcast.9), channel_id=1, source_target_pairs={{0,4},{4,8},{8,12},{12,16},{16,20},{20,24},{24,28},{1,5},{5,9},{9,... | collective-permute-start | bytes 1572872 | tf_op jit(solution)/shard_map/ppermute | solution.py:412
  9.1 0.7 copy-start.1
  9.8 1.0 %copy-start.2 = (f32[1,1,32,4096]{3,2,1,0:T(8,128)S(1)}, f32[1,1,32,4096]{3,2,1,0:T(8,128)}, u32[]{:S(2)}) copy-start(f32[1,1,32,4096]{3,2,1,0:T(8,128)} %param.6) | copy-start | bytes 1572868
  10.8 2.0 %copy-start = (f32[1,1,32,4096]{3,2,1,0:T(8,128)S(1)}, f32[1,1,32,4096]{3,2,1,0:T(8,128)}, u32[]{:S(2)}) copy-start(f32[1,1,32,4096]{3,2,1,0:T(8,128)} %param.7) | copy-start | bytes 1572868
  10.8 42.0 %copy-start.3 = (f32[1,1,32,4096]{3,2,1,0:T(8,128)S(1)}, f32[1,1,32,4096]{3,2,1,0:T(8,128)}, u32[]{:S(2)}) copy-start(f32[1,1,32,4096]{3,2,1,0:T(8,128)} %param.6) | copy-start | bytes 1572868
  12.8 42.1 %collective-permute-start.4 = (f32[32,4096]{1,0:T(8,128)S(1)}, f32[32,4096]{1,0:T(8,128)S(1)}, u32[]{:S(2)}, u32[]{:S(2)}) collective-permute-start(f32[32,4096]{1,0:T(8,128)S(1)} %bitcast.7), channel_id=1, source_target_pairs={{4,0},{8,4},{12,8},{16,12},{20,16},{24,20},{28,24},{5,1},{9,5},{13... | collective-permute-start | bytes 1572872 | tf_op jit(solution)/shard_map/ppermute | solution.py:412
  14.1 22.6 %collective-permute-start.3 = (f32[8,33,32]{2,1,0:T(8,128)S(1)}, f32[8,33,32]{2,1,0:T(8,128)S(1)}, u32[]{:S(2)}, u32[]{:S(2)}) collective-permute-start(f32[8,33,32]{2,1,0:T(8,128)S(1)} %pad_maximum_fusion.p_ref), channel_id=1, source_target_pairs={{0,4},{4,8},{8,12},{12,16},{16,20},{20,24},{24,28},{1,5},{5,9},{9,... | collective-permute-start | bytes 101384 | tf_op jit(solution)/shard_map/ppermute | solution.py:412
  19.6 11.1 %collective-permute-start.1 = (f32[1,33,32]{2,1,0:T(8,128)S(1)}, f32[1,33,32]{2,1,0:T(8,128)S(1)}, u32[]{:S(2)}, u32[]{:S(2)}) collective-permute-start(f32[1,33,32]{2,1,0:T(8,128)S(1)} %slice.9), channel_id=1, source_target_pairs={{8,0},{9,1},{10,2},{11,3}} | collective-permute-start | bytes 12680 | tf_op jit(solution)/shard_map/ppermute | solution.py:450
  36.7 14.2 %collective-permute-start.5 = (f32[32,1664]{1,0:T(8,128)S(1)}, f32[32,1664]{1,0:T(8,128)S(1)}, u32[]{:S(2)}, u32[]{:S(2)}) collective-permute-start(f32[32,1664]{1,0:T(8,128)S(1)} %get-tuple-element.57), channel_id=1, source_target_pairs={{0,8},{4,12},{8,16},{12,20},{1,9},{5,13},{9,17},{13,21},{2,10},{6,... | collective-permute-start | bytes 638984 | tf_op jit(solution)/shard_map/ppermute | solution.py:466
  40.2 20.9 %collective-permute-start.6 = (f32[32,1664]{1,0:T(8,128)S(1)}, f32[32,1664]{1,0:T(8,128)S(1)}, u32[]{:S(2)}, u32[]{:S(2)}) collective-permute-start(f32[32,1664]{1,0:T(8,128)S(1)} %get-tuple-element.58), channel_id=1, source_target_pairs={{4,8},{8,12},{12,16},{16,20},{5,9},{9,13},{13,17},{17,21},{6,10},{... | collective-permute-start | bytes 638984 | tf_op jit(solution)/shard_map/ppermute | solution.py:466
  40.9 20.3 %collective-permute-start.7 = (f32[32,1664]{1,0:T(8,128)S(1)}, f32[32,1664]{1,0:T(8,128)S(1)}, u32[]{:S(2)}, u32[]{:S(2)}) collective-permute-start(f32[32,1664]{1,0:T(8,128)S(1)} %get-tuple-element.59), channel_id=1, source_target_pairs={{12,8},{16,12},{20,16},{0,20},{13,9},{17,13},{21,17},{1,21},{14,10... | collective-permute-start | bytes 638984 | tf_op jit(solution)/shard_map/ppermute | solution.py:466
  45.8 15.4 %collective-permute-start.8 = (f32[32,1664]{1,0:T(8,128)S(1)}, f32[32,1664]{1,0:T(8,128)S(1)}, u32[]{:S(2)}, u32[]{:S(2)}) collective-permute-start(f32[32,1664]{1,0:T(8,128)S(1)} %get-tuple-element.60), channel_id=1, source_target_pairs={{16,8},{20,12},{0,16},{4,20},{17,9},{21,13},{1,17},{5,21},{18,10},... | collective-permute-start | bytes 638984 | tf_op jit(solution)/shard_map/ppermute | solution.py:466
  51.0 10.2 %collective-permute-start.9 = (f32[32,1664]{1,0:T(8,128)S(1)}, f32[32,1664]{1,0:T(8,128)S(1)}, u32[]{:S(2)}, u32[]{:S(2)}) collective-permute-start(f32[32,1664]{1,0:T(8,128)S(1)} %get-tuple-element.62), channel_id=1, source_target_pairs={{20,8},{0,12},{4,16},{8,20},{21,9},{1,13},{5,17},{9,21},{22,10},{2... | collective-permute-start | bytes 638984 | tf_op jit(solution)/shard_map/ppermute | solution.py:466
  61.9 25.1 %collective-permute-start.10 = (f32[32,1024]{1,0:T(8,128)S(1)}, f32[32,1024]{1,0:T(8,128)S(1)}, u32[]{:S(2)}, u32[]{:S(2)}) collective-permute-start(f32[32,1024]{1,0:T(8,128)S(1)} %get-tuple-element.64), channel_id=1, source_target_pairs={{8,12},{12,16},{16,20},{20,24},{0,8},{9,13},{13,17},{17,21},{21,25... | collective-permute-start | bytes 393224 | tf_op jit(solution)/shard_map/ppermute | solution.py:489
  72.8 17.3 %collective-permute-start.11 = (f32[32,1024]{1,0:T(8,128)S(1)}, f32[32,1024]{1,0:T(8,128)S(1)}, u32[]{:S(2)}, u32[]{:S(2)}) collective-permute-start(f32[32,1024]{1,0:T(8,128)S(1)} %get-tuple-element.65), channel_id=1, source_target_pairs={{8,16},{12,20},{16,24},{20,28},{0,8},{9,17},{13,21},{17,25},{21,29... | collective-permute-start | bytes 393224 | tf_op jit(solution)/shard_map/ppermute | solution.py:489
  74.7 15.3 %collective-permute-start.12 = (f32[32,1024]{1,0:T(8,128)S(1)}, f32[32,1024]{1,0:T(8,128)S(1)}, u32[]{:S(2)}, u32[]{:S(2)}) collective-permute-start(f32[32,1024]{1,0:T(8,128)S(1)} %get-tuple-element.66), channel_id=1, source_target_pairs={{8,20},{12,24},{16,28},{20,12},{0,8},{9,21},{13,25},{17,29},{21,13... | collective-permute-start | bytes 393224 | tf_op jit(solution)/shard_map/ppermute | solution.py:489
  84.4 5.6 %collective-permute-start.13 = (f32[32,1024]{1,0:T(8,128)S(1)}, f32[32,1024]{1,0:T(8,128)S(1)}, u32[]{:S(2)}, u32[]{:S(2)}) collective-permute-start(f32[32,1024]{1,0:T(8,128)S(1)} %get-tuple-element.67), channel_id=1, source_target_pairs={{8,24},{12,28},{16,12},{20,16},{0,8},{9,25},{13,29},{17,13},{21,17... | collective-permute-start | bytes 393224 | tf_op jit(solution)/shard_map/ppermute | solution.py:489
  86.3 3.7 %collective-permute-start.14 = (f32[32,1024]{1,0:T(8,128)S(1)}, f32[32,1024]{1,0:T(8,128)S(1)}, u32[]{:S(2)}, u32[]{:S(2)}) collective-permute-start(f32[32,1024]{1,0:T(8,128)S(1)} %get-tuple-element.63.local_ref), channel_id=1, source_target_pairs={{8,28},{9,29},{10,30},{11,31}} | collective-permute-start | bytes 393224 | tf_op jit(solution)/shard_map/ppermute | solution.py:489
  87.0 1.4 %collective-permute-start.15 = (f32[8,32,33]{2,1,0:T(8,128)S(1)}, f32[8,32,33]{2,1,0:T(8,128)S(1)}, u32[]{:S(2)}, u32[]{:S(2)}) collective-permute-start(f32[8,32,33]{2,1,0:T(8,128)S(1)} %get-tuple-element.69._), channel_id=1, source_target_pairs={{0,1},{1,0},{2,3},{3,2},{4,5},{5,4},{6,7},{7,6},{8,9},{9,8},{10,11... | collective-permute-start | bytes 101384 | tf_op jit(solution)/shard_map/ppermute | solution.py:421
  88.4 5.6 %collective-permute-start.16 = (f32[8,32,33]{2,1,0:T(8,128)S(1)}, f32[8,32,33]{2,1,0:T(8,128)S(1)}, u32[]{:S(2)}, u32[]{:S(2)}) collective-permute-start(f32[8,32,33]{2,1,0:T(8,128)S(1)} %add.6), channel_id=1, source_target_pairs={{0,2},{1,3},{2,0},{3,1},{4,6},{5,7},{6,4},{7,5},{8,10},{9,11},{10,... | collective-permute-start | bytes 101384 | tf_op jit(solution)/shard_map/ppermute | solution.py:421
  94.1 0.8 copy-start.4
